TPU v7x, 128 devices: a whole 4x4x4 slice. The times are simulated.
128 devices in a mesh: dp: 4 (over x), ctx: 16 (over z, y), head: 2 (over core).
Axes of the slice: x: 4, y: 4, z: 4, core: 2. Of those that a mesh axis runs over, the one named last changes fastest.
Arguments:
- queries: bfloat16 [16384, 32, 128], P(('dp', 'ctx'), 'head'), parts along dimension 0, may hold values from -112 to 112, as said below
- keys: bfloat16 [16384, 16, 128], P(('dp', 'ctx'), 'head'), parts along dimension 0, may hold values from -4 to 4, as said below
- values: bfloat16 [16384, 16, 128], P(('dp', 'ctx'), 'head'), parts along dimension 0, may hold values from -4 to 4
- out_grad: bfloat16 [16384, 32, 128], P(('dp', 'ctx'), 'head'), parts along dimension 0, may hold values from -4 to 4
- doc_lengths: int32 [128], P('dp'), parts along dimension 0, may hold values from 1 to 1024, 4096 in all
Outputs:
- attended: bfloat16 [16384, 32, 128], P(('dp', 'ctx'), 'head'), parts along dimension 0
- query_grad: bfloat16 [16384, 32, 128], P(('dp', 'ctx'), 'head'), parts along dimension 0
- key_grad: bfloat16 [16384, 16, 128], P(('dp', 'ctx'), 'head'), parts along dimension 0
- value_grad: bfloat16 [16384, 16, 128], P(('dp', 'ctx'), 'head'), parts along dimension 0
There are 4 independent parts, one for each index of `dp`. A program takes and returns all parts, laid end to end along the dimension named above; each array names one. Nothing has to cross between parts.
Inputs may be any that keep to these rules, and one draw needn't show every extreme that they name: Entries of the queries lie in this range. Entries of the keys lie in this range. `doc_lengths`: the lengths sum to 4096; the longest document has exactly 1024 tokens.
All inputs are finite; a program needn't handle non-finite values.
Results may differ from a plain program's by a relative error of at most 0.0055.
Values may be sent and summed in bfloat16 or wider, within the bound.
No kernel may reach another device: no remote copies, remote signals or barrier semaphores. Data moves between devices by JAX's collectives and lax.ppermute only.
A program may use at most 192 MiB of HBM per device.

v0:
```python
import functools

import jax
import jax.numpy as jnp
from jax import lax
from jax.experimental import pallas as pl
from jax.experimental.pallas import tpu as pltpu
from jax.sharding import PartitionSpec as P

WINDOW = 1024
SCALING = 168.0 ** (-0.5)
LOG2E = 1.4426950408889634
NEG = -1e30

NT = (((1,), (1,)), ((), ()))
NN = (((1,), (0,)), ((), ()))


def dot(a, b, dims):
    return lax.dot_general(a, b, dims, preferred_element_type=jnp.float32)


def attention_kernel(first_ref, ends_ref, x_ref, y_ref, kt_ref, vt_ref, dk_ref, dv_ref, s_ref, g_ref, *, blocks, rows):
    dk_ref[...] = jnp.zeros_like(dk_ref)
    dv_ref[...] = jnp.zeros_like(dv_ref)
    diff = lax.broadcasted_iota(jnp.int32, (rows, rows), 1) - lax.broadcasted_iota(jnp.int32, (rows, rows), 0)

    def transpose_step(t, carry):
        kt_ref[t] = x_ref[t, 2].T
        vt_ref[t] = x_ref[t, 3].T
        return carry

    lax.fori_loop(0, blocks, transpose_step, 0)

    def query_step(i, carry):
        q = x_ref[i, 0]
        do = x_ref[i, 1]
        first = first_ref[i]
        count = i - first + 1
        pos = i * rows + lax.broadcasted_iota(jnp.int32, (1, rows), 1)
        ends = ends_ref[...]
        start = jnp.max(jnp.where(ends <= pos, ends, 0), axis=0, keepdims=True)
        reach = pos - jnp.maximum(start, pos - (WINDOW - 1))

        def score_step(t, top):
            raw = dot(x_ref[first + t, 2], q, NT)
            gap = diff + (i - first - t) * rows
            raw = jnp.where((gap >= 0) & (gap <= reach), raw, NEG)
            s_ref[t] = raw
            return jnp.maximum(top, jnp.max(raw, axis=0, keepdims=True))

        top = lax.fori_loop(0, count, score_step, jnp.full((1, rows), NEG, jnp.float32))

        def weight_step(t, sums):
            total, mixed = sums
            p = jnp.exp2((s_ref[t] - top) * (SCALING * LOG2E))
            g = dot(x_ref[first + t, 3], do, NT)
            s_ref[t] = p
            g_ref[t] = g
            return (
                total + jnp.sum(p, axis=0, keepdims=True),
                mixed + jnp.sum(p * g, axis=0, keepdims=True),
            )

        zero = jnp.zeros((1, rows), jnp.float32)
        total, mixed = lax.fori_loop(0, count, weight_step, (zero, zero))
        inverse = 1.0 / total
        row_total = mixed * inverse

        def grad_step(t, sums):
            out, dq = sums
            w = s_ref[t] * inverse
            wb = w.astype(jnp.bfloat16)
            ds = (w * (g_ref[t] - row_total)).astype(jnp.bfloat16)
            out = out + dot(vt_ref[first + t], wb, NN)
            dq = dq + dot(kt_ref[first + t], ds, NN)
            dv_ref[first + t] += dot(wb, do, NN)
            dk_ref[first + t] += dot(ds, q, NN)
            return out, dq

        zeros = jnp.zeros((q.shape[1], rows), jnp.float32)
        out, dq = lax.fori_loop(0, count, grad_step, (zeros, zeros))
        y_ref[i, 0] = out.T.astype(jnp.bfloat16)
        y_ref[i, 1] = (SCALING * dq).T.astype(jnp.bfloat16)
        return carry

    lax.fori_loop(0, blocks, query_step, 0)

    def write_step(t, carry):
        y_ref[t, 2] = (SCALING * dk_ref[t]).astype(jnp.bfloat16)
        y_ref[t, 3] = dv_ref[t].astype(jnp.bfloat16)
        return carry

    lax.fori_loop(0, blocks, write_step, 0)


def attention(first, ends, x):
    blocks, _, rows, dim = x.shape
    tiles = WINDOW // rows + 1
    return pl.pallas_call(
        functools.partial(attention_kernel, blocks=blocks, rows=rows),
        out_shape=jax.ShapeDtypeStruct(x.shape, jnp.bfloat16),
        in_specs=[
            pl.BlockSpec(memory_space=pltpu.SMEM),
            pl.BlockSpec(memory_space=pltpu.VMEM),
            pl.BlockSpec(memory_space=pltpu.VMEM),
        ],
        out_specs=pl.BlockSpec(memory_space=pltpu.VMEM),
        scratch_shapes=[
            pltpu.VMEM((blocks, dim, rows), jnp.bfloat16),
            pltpu.VMEM((blocks, dim, rows), jnp.bfloat16),
            pltpu.VMEM((blocks, rows, dim), jnp.float32),
            pltpu.VMEM((blocks, rows, dim), jnp.float32),
            pltpu.VMEM((tiles, rows, rows), jnp.float32),
            pltpu.VMEM((tiles, rows, rows), jnp.float32),
        ],
        compiler_params=pltpu.CompilerParams(vmem_limit_bytes=40 * 1024 * 1024),
        cost_estimate=pl.CostEstimate(flops=3 * 10**9, bytes_accessed=8 * 2**20, transcendentals=4 * 10**6),
    )(first, ends, x)


def body(queries, keys, values, out_grad, doc_lengths):
    rows, heads, dim = queries.shape
    kv_heads = keys.shape[1]
    group = heads // kv_heads
    blocks = lax.axis_size("ctx")
    docs = doc_lengths.shape[0]
    upto = jnp.arange(docs)[:, None] >= jnp.arange(docs)[None, :]
    ends = jnp.sum(jnp.where(upto, doc_lengths[None, :], 0), axis=1)
    heads_pos = jnp.arange(blocks, dtype=jnp.int32) * rows
    start = jnp.max(jnp.where(ends[None, :] <= heads_pos[:, None], ends[None, :], 0), axis=1)
    first = jnp.maximum(start, heads_pos - (WINDOW - 1)) // rows
    first = jnp.maximum(first, 0).astype(jnp.int32)

    def by_head(array, copies):
        array = jnp.swapaxes(array, 0, 1)
        return jnp.repeat(array, copies, axis=0) if copies > 1 else array

    packed = jnp.stack(
        (by_head(queries, 1), by_head(out_grad, 1), by_head(keys, group), by_head(values, group)), 1
    )
    x = lax.all_to_all(packed, "ctx", 0, 0)
    y = attention(first, ends[:, None].astype(jnp.int32), x)
    back = lax.all_to_all(y, "ctx", 0, 0)
    attended = jnp.swapaxes(back[:, 0], 0, 1)
    query_grad = jnp.swapaxes(back[:, 1], 0, 1)
    kv = back[:, 2:].astype(jnp.float32).reshape(kv_heads, group, 2, rows, dim).sum(1)
    kv = jnp.swapaxes(kv, 0, 2).astype(jnp.bfloat16)
    return attended, query_grad, kv[:, 0], kv[:, 1]


def solution(mesh):
    spec = P(("dp", "ctx"), "head", None)
    return jax.shard_map(
        body,
        mesh=mesh,
        in_specs=(spec, spec, spec, spec, P("dp")),
        out_specs=(spec, spec, spec, spec),
        check_vma=False,
    )
```

profile of v0, /device:TPU:1, one launch (start us, length us, event | category | flops | bytes accessed | tf_op | source)
XLA Modules:
  0.0 175.4 jit_solution(8116929030711573769)
XLA Ops:
  0.6 1.1 copy.27
  1.7 1.1 copy.28
  2.9 2.1 %copy_bitcast_fusion = (bf16[16,1,256,128]{3,2,1,0:T(8,128)(2,1)S(1)}, bf16[16,1,256,128]{3,2,1,0:T(8,128)(2,1)S(1)}) fusion(bf16[256,16,128]{2,1,0:T(8,128)(2,1)} %param.8, bf16[256,16,128]{2,1,0:T(8,128)(2,1)} %param.5), kind=kLoop, calls=%fused_computation.4 | loop fusion | bytes 4194304 | tf_op jit(solution)/shard_map/stack | solution.py:139
  4.9 0.2 broadcast_in_dim.41
  5.2 0.2 broadcast_in_dim.42
  5.4 2.3 %pad_maximum_fusion = bf16[16,4,256,128]{3,2,1,0:T(8,128)(2,1)} fusion(bf16[16,1,256,128]{3,2,1,0:T(8,128)(2,1)S(1)} %bitcast.30, bf16[16,1,256,128]{3,2,1,0:T(8,128)(2,1)S(1)} %bitcast.29, bf16[16,1,256,128]{3,2,1,0:T(8,128)(2,1)S(1)} %get-tuple-element.20, bf16[16,1,256,128]{3,2,1,0:T(8,128)(2,1)S(1)} %get-tuple-element.21), kind=kLoop, calls=%fused_computation | loop fusion | flops 6291456 | bytes 8388608 | tf_op jit(solution)/shard_map/stack | solution.py:139
  7.6 0.0 copy-start
  7.6 8.8 %all-to-all-start = ((bf16[16,4,256,128]{3,2,1,0:T(8,128)(2,1)}), bf16[16,4,256,128]{3,2,1,0:T(8,128)(2,1)}, u32[]{:S(2)}, u32[]{:S(2)}) async-start(bf16[16,4,256,128]{3,2,1,0:T(8,128)(2,1)} %pad_maximum_fusion), calls=%async_computation | async-start | bytes 8388608 | tf_op jit(solution)/shard_map/all_to_all | solution.py:142
  16.4 0.0 copy-done
  16.4 0.1 select_reduce_fusion
  16.5 0.1 copy.29.ends_ref
  16.6 0.2 select_reduce_fusion.1
  16.8 61.9 %all-to-all-done.x_ref = bf16[16,4,256,128]{3,2,1,0:T(8,128)(2,1)} async-done(((bf16[16,4,256,128]{3,2,1,0:T(8,128)(2,1)}), bf16[16,4,256,128]{3,2,1,0:T(8,128)(2,1)}, u32[]{:S(2)}, u32[]{:S(2)}) %all-to-all-start) | async-done | bytes 4194336 | tf_op jit(solution)/shard_map/all_to_all | solution.py:142
  78.8 35.8 %shard_map.84 = bf16[16,4,256,128]{3,2,1,0:T(8,128)(2,1)S(1)} custom-call(s32[16]{0:T(128)S(1)} %fusion.first_ref, s32[32,1]{1,0:T(8,128)S(1)} %copy.29.ends_ref, bf16[16,4,256,128]{3,2,1,0:T(8,128)(2,1)} %all-to-all-done.x_ref), custom_call_target="tpu_custom_call" | custom-call | flops 3000000000 | bytes 8388608 | tf_op jit(solution)/shard_map/pallas_call | solution.py:100
  114.6 54.6 %all_to_all.10 = bf16[16,4,256,128]{3,2,1,0:T(8,128)(2,1)S(1)} all-to-all(bf16[16,4,256,128]{3,2,1,0:T(8,128)(2,1)S(1)} %shard_map.84), channel_id=1, replica_groups=mesh['dp'=4,'ctx'=16,'head'=2] {'ctx'}, dimensions={0} | all-to-all | bytes 8388608 | tf_op jit(solution)/shard_map/all_to_all | solution.py:144
  169.2 0.2 slice_bitcast_fusion
  169.4 1.6 copy.30
  171.0 1.6 copy.31
  172.7 0.4 bitcast_reduce_fusion
  173.1 0.1 slice_bitcast_fusion.2
  173.2 1.1 copy.32
  174.3 1.1 copy.33
  (2 shorter events, 0.0 us)
Async XLA Ops:
  7.6 8.8 %copy-start = (s32[32]{0:T(128)S(1)}, s32[32]{0:T(128)}, u32[]{:S(2)}) copy-start(s32[32]{0:T(128)} %param.9) | copy-start | bytes 388
  7.6 71.1 %all-to-all-start = ((bf16[16,4,256,128]{3,2,1,0:T(8,128)(2,1)}), bf16[16,4,256,128]{3,2,1,0:T(8,128)(2,1)}, u32[]{:S(2)}, u32[]{:S(2)}) async-start(bf16[16,4,256,128]{3,2,1,0:T(8,128)(2,1)} %pad_maximum_fusion), calls=%async_computation | async-start | bytes 8388608 | tf_op jit(solution)/shard_map/all_to_all | solution.py:142
where the time goes:
time: 178 us; the launch traced here: 175 us
  waiting for transfers between devices  61.9 us (35%)
  blocking collectives  54.6 us (31%)
  Pallas kernels  35.8 us (20%)
  local copies, waits for them, and re-layouts  10.6 us (6%)
  starting transfers between devices  8.78 us (5%)
  other arithmetic  2.97 us (2%)
    all_to_all x1, waiting for transfers between devices, body(): x = lax.all_to_all(packed, 'ctx', 0, 0)  61.9 us
    all_to_all x1, blocking collectives, body(): back = lax.all_to_all(y, 'ctx', 0, 0)  54.6 us
    pallas_call x1, Pallas kernels, attention(): pl.pallas_call(functools.partial(attention_kernel, blocks=blocks, rows=ro...  35.8 us
    all_to_all x1, starting transfers between devices, body(): x = lax.all_to_all(packed, 'ctx', 0, 0)  8.78 us
    unnamed x6, local copies, waits for them, and re-layouts  5.57 us
  transfers between devices with their start and end apart: 1, of which 1 were waited for; matrix products, arithmetic and copies ran while one was open for 0% of the time, Pallas kernels for 0%

commit v1 on v0

v1 whole, which is shorter than its diff:
```python
import functools

import jax
import jax.numpy as jnp
from jax import lax
from jax.experimental import pallas as pl
from jax.experimental.pallas import tpu as pltpu
from jax.sharding import PartitionSpec as P

WINDOW = 1024
SCALING = 168.0 ** (-0.5)
LOG2E = 1.4426950408889634
NEG = -1e30

NT = (((1,), (1,)), ((), ()))
NN = (((1,), (0,)), ((), ()))


def dot(a, b, dims):
    return lax.dot_general(a, b, dims, preferred_element_type=jnp.float32)


def attention_kernel(
    meta_ref, ends_ref, kv_ref, halo_ref, x_ref, y_ref, dkv_ref, dhalo_ref, k_ref, kt_ref, acc_ref, s_ref, g_ref,
    *, blocks, reach_back, rows, group,
):
    dim = x_ref.shape[3]
    wide = group * rows

    def halo_step(t, carry):
        for n in range(2):
            tile = halo_ref[t, n]
            k_ref[t, n] = tile
            kt_ref[t, n] = tile.T
            acc_ref[t, n] = jnp.zeros((rows, dim), jnp.float32)
        return carry

    def copy_step(t, carry):
        for n in range(2):
            tile = kv_ref[t, n]
            k_ref[reach_back + t, n] = tile
            kt_ref[reach_back + t, n] = tile.T
        return carry

    lax.fori_loop(0, reach_back, halo_step, 0)
    lax.fori_loop(0, blocks, copy_step, 0, unroll=2)

    lane = lax.rem(lax.broadcasted_iota(jnp.int32, (1, wide), 1), rows)
    diff = lane - lax.broadcasted_iota(jnp.int32, (rows, wide), 0)

    def query_tile(i, count):
        own = i + reach_back
        first = own - (count - 1)
        q = x_ref[i, 0:group].reshape(wide, dim)
        do = x_ref[i, group:2 * group].reshape(wide, dim)
        pos = meta_ref[blocks] + i * rows + lane
        ends = ends_ref[...]
        start = jnp.max(jnp.where(ends <= pos, ends, 0), axis=0, keepdims=True)
        reach = pos - jnp.maximum(start, pos - (WINDOW - 1))
        top = None
        for t in range(count):
            raw = dot(k_ref[first + t, 0], q, NT)
            offset = (count - 1 - t) * rows
            keep = diff <= reach - offset
            if offset == 0:
                keep = keep & (diff >= 0)
            raw = jnp.where(keep, raw, NEG)
            s_ref[t] = raw
            here = jnp.max(raw, axis=0, keepdims=True)
            top = here if top is None else jnp.maximum(top, here)
            g_ref[t] = dot(k_ref[first + t, 1], do, NT)
        total = mixed = 0.0
        for t in range(count):
            p = jnp.exp2((s_ref[t] - top) * (SCALING * LOG2E))
            s_ref[t] = p
            total += jnp.sum(p, axis=0, keepdims=True)
            mixed += jnp.sum(p * g_ref[t], axis=0, keepdims=True)
        inverse = 1.0 / total
        row_total = mixed * inverse
        out = dq = 0.0
        for t in range(count):
            w = s_ref[t] * inverse
            wb = w.astype(jnp.bfloat16)
            ds = (w * (g_ref[t] - row_total)).astype(jnp.bfloat16)
            out += dot(kt_ref[first + t, 1], wb, NN)
            dq += dot(kt_ref[first + t, 0], ds, NN)
            if t == count - 1:
                acc_ref[own, 1] = dot(wb, do, NN)
                acc_ref[own, 0] = dot(ds, q, NN)
            else:
                acc_ref[first + t, 1] += dot(wb, do, NN)
                acc_ref[first + t, 0] += dot(ds, q, NN)
        for n in range(group):
            y_ref[i, n] = out[:, n * rows:(n + 1) * rows].T.astype(jnp.bfloat16)
            y_ref[i, group + n] = (SCALING * dq[:, n * rows:(n + 1) * rows]).T.astype(jnp.bfloat16)

    def query_step(i, carry):
        count = meta_ref[i]
        for n in range(1, reach_back + 2):
            pl.when(count == n)(functools.partial(query_tile, i, n))
        return carry

    lax.fori_loop(0, blocks, query_step, 0)

    for t in range(reach_back):
        dhalo_ref[t, 0] = (SCALING * acc_ref[t, 0]).astype(jnp.bfloat16)
        dhalo_ref[t, 1] = acc_ref[t, 1].astype(jnp.bfloat16)

    def write_step(t, carry):
        dkv_ref[t, 0] = SCALING * acc_ref[reach_back + t, 0]
        dkv_ref[t, 1] = acc_ref[reach_back + t, 1]
        return carry

    lax.fori_loop(0, blocks, write_step, 0, unroll=2)


def attention(meta, ends, kv, halo, x):
    blocks, _, rows, dim = kv.shape
    reach_back = halo.shape[0]
    group = x.shape[1] // 2
    vmem = pl.BlockSpec(memory_space=pltpu.VMEM)
    return pl.pallas_call(
        functools.partial(attention_kernel, blocks=blocks, reach_back=reach_back, rows=rows, group=group),
        out_shape=(
            jax.ShapeDtypeStruct(x.shape, jnp.bfloat16),
            jax.ShapeDtypeStruct(kv.shape, jnp.float32),
            jax.ShapeDtypeStruct(halo.shape, jnp.bfloat16),
        ),
        in_specs=[pl.BlockSpec(memory_space=pltpu.SMEM), vmem, vmem, vmem, vmem],
        out_specs=(vmem, vmem, vmem),
        scratch_shapes=[
            pltpu.VMEM((reach_back + blocks, 2, rows, dim), jnp.bfloat16),
            pltpu.VMEM((reach_back + blocks, 2, dim, rows), jnp.bfloat16),
            pltpu.VMEM((reach_back + blocks, 2, rows, dim), jnp.float32),
            pltpu.VMEM((reach_back + 1, rows, group * rows), jnp.float32),
            pltpu.VMEM((reach_back + 1, rows, group * rows), jnp.float32),
        ],
        compiler_params=pltpu.CompilerParams(vmem_limit_bytes=40 * 1024 * 1024),
        cost_estimate=pl.CostEstimate(flops=5 * 10**9, bytes_accessed=8 * 2**20, transcendentals=4 * 10**6),
    )(meta, ends, kv, halo, x)


def body(queries, keys, values, out_grad, doc_lengths):
    rows, heads, dim = queries.shape
    kv_heads = keys.shape[1]
    group = heads // kv_heads
    devices = lax.axis_size("ctx")
    parts = devices // kv_heads
    reach_back = WINDOW // rows
    where = lax.axis_index("ctx") // kv_heads
    groups = [[p * kv_heads + j for j in range(kv_heads)] for p in range(parts)]
    onward = [(p * kv_heads + j, (p + 1) * kv_heads + j) for p in range(parts - 1) for j in range(kv_heads)]

    docs = doc_lengths.shape[0]
    upto = jnp.arange(docs)[:, None] >= jnp.arange(docs)[None, :]
    ends = jnp.sum(jnp.where(upto, doc_lengths[None, :], 0), axis=1)
    tile = where * kv_heads + jnp.arange(kv_heads, dtype=jnp.int32)
    start = jnp.max(jnp.where(ends[None, :] <= tile[:, None] * rows, ends[None, :], 0), axis=1)
    first = jnp.maximum(start, tile * rows - (WINDOW - 1))
    count = tile - jnp.maximum(first, 0) // rows + 1
    meta = jnp.concatenate((count, (where * kv_heads * rows)[None])).astype(jnp.int32)

    def exchange(array):
        return lax.all_to_all(array, "ctx", 0, 0, axis_index_groups=groups)

    kv = exchange(jnp.stack((jnp.swapaxes(keys, 0, 1), jnp.swapaxes(values, 0, 1)), 1))
    halo = lax.ppermute(kv[kv_heads - reach_back:], "ctx", onward)
    x = jnp.concatenate(
        [jnp.swapaxes(a, 0, 1).reshape(kv_heads, group, rows, dim) for a in (queries, out_grad)], 1
    )
    x = exchange(x)
    y, dkv, dhalo = attention(meta, ends[:, None].astype(jnp.int32), kv, halo, x)
    dhalo = lax.ppermute(dhalo, "ctx", [(b, a) for a, b in onward])
    y = exchange(y)
    still = kv_heads - reach_back
    dkv = jnp.concatenate((dkv[:still], dkv[still:] + dhalo.astype(jnp.float32)), 0).astype(jnp.bfloat16)
    dkv = exchange(dkv)
    attended = jnp.swapaxes(y[:, :group].reshape(heads, rows, dim), 0, 1)
    query_grad = jnp.swapaxes(y[:, group:].reshape(heads, rows, dim), 0, 1)
    return attended, query_grad, jnp.swapaxes(dkv[:, 0], 0, 1), jnp.swapaxes(dkv[:, 1], 0, 1)


def solution(mesh):
    spec = P(("dp", "ctx"), "head", None)
    return jax.shard_map(
        body,
        mesh=mesh,
        in_specs=(spec, spec, spec, spec, P("dp")),
        out_specs=(spec, spec, spec, spec),
        check_vma=False,
    )
```

time: 178 us -> 152 us (0.85)
  blocking collectives: 54.6 us -> 19.9 us
  Pallas kernels: 35.8 us -> 13.1 us
  waiting for transfers between devices: 61.9 us -> 82.7 us
  starting transfers between devices: 8.78 us -> 20.4 us
    ppermute x0 -> x2, waiting for transfers between devices: none -> 44.6 us  [the longest x1 28.3 us: body(): halo = lax.ppermute(kv[kv_heads - reach_back:], 'ctx', onward)]
    all_to_all x1, blocking collectives: 54.6 us -> 19.9 us  [exchange(): return lax.all_to_all(array, 'ctx', 0, 0, axis_index_groups=groups)]
    all_to_all x1 -> x3, waiting for transfers between devices: 61.9 us -> 38.2 us  [exchange(): return lax.all_to_all(array, 'ctx', 0, 0, axis_index_groups=groups)]
    pallas_call x1, Pallas kernels: 35.8 us -> 13.1 us  [attention(): pl.pallas_call(functools.partial(attention_kernel, blocks=blocks, reach_b...]
    ppermute x0 -> x2, starting transfers between devices: none -> 6.53 us  [the longest x1 5.24 us: body(): halo = lax.ppermute(kv[kv_heads - reach_back:], 'ctx', onward)]
    all_to_all x1 -> x3, starting transfers between devices: 8.78 us -> 13.9 us  [exchange(): return lax.all_to_all(array, 'ctx', 0, 0, axis_index_groups=groups)]
    reshape x0 -> x2, local copies, waits for them, and re-layouts: none -> 3.3 us  [the longest x1 1.65 us: body(): query_grad = jnp.swapaxes(y[:, group:].reshape(heads, rows, dim), 0, 1)]
    transpose x3, local copies, waits for them, and re-layouts: 2.41 us -> 0.61 us  [the longest x2 0.54 us: body(): jnp.swapaxes(a, 0, 1).reshape(kv_heads, group, rows, dim)]
  transfers between devices with their start and end apart: 1 -> 5, of which waited for: 1 -> 4; matrix products, arithmetic and copies ran while one was open for 0% -> 3% of each run, Pallas kernels for 0% -> 0%
where the time goes in v1:
time: 152 us; the launch traced here: 150 us
  waiting for transfers between devices  82.7 us (54%)
  starting transfers between devices  20.4 us (13%)
  blocking collectives  19.9 us (13%)
  Pallas kernels  13.1 us (9%)
  local copies, waits for them, and re-layouts  9.78 us (6%)
  other arithmetic  3.18 us (2%)
    all_to_all x3, waiting for transfers between devices, exchange(): return lax.all_to_all(array, 'ctx', 0, 0, axis_index_groups=groups)  38.2 us
    ppermute x1, waiting for transfers between devices, body(): halo = lax.ppermute(kv[kv_heads - reach_back:], 'ctx', onward)  28.3 us
    all_to_all x1, blocking collectives, exchange(): return lax.all_to_all(array, 'ctx', 0, 0, axis_index_groups=groups)  19.9 us
    ppermute x1, waiting for transfers between devices, body(): dhalo = lax.ppermute(dhalo, 'ctx', [(b, a) for a, b in onward])  16.3 us
    all_to_all x3, starting transfers between devices, exchange(): return lax.all_to_all(array, 'ctx', 0, 0, axis_index_groups=groups)  13.9 us
    pallas_call x1, Pallas kernels, attention(): pl.pallas_call(functools.partial(attention_kernel, blocks=blocks, reach_b...  13.1 us
    ppermute x1, starting transfers between devices, body(): halo = lax.ppermute(kv[kv_heads - reach_back:], 'ctx', onward)  5.24 us
    unnamed x14, local copies, waits for them, and re-layouts  4.12 us
  transfers between devices with their start and end apart: 5, of which 4 were waited for; matrix products, arithmetic and copies ran while one was open for 3% of the time, Pallas kernels for 0%

profile of v1, /device:TPU:1, one launch (start us, length us, event | category | flops | bytes accessed | tf_op | source)
XLA Modules:
  0.0 149.9 jit_solution(604295844768735011)
XLA Ops:
  0.6 1.4 copy_bitcast_fusion.2
  2.0 0.0 copy-start.3
  2.0 1.1 pad_maximum_fusion.1
  3.1 0.0 copy-start.4
  3.1 6.5 %all-to-all-start = ((bf16[8,2,256,128]{3,2,1,0:T(8,128)(2,1)}), bf16[8,2,256,128]{3,2,1,0:T(8,128)(2,1)S(1)}, u32[]{:S(2)}, u32[]{:S(2)}) async-start(bf16[8,2,256,128]{3,2,1,0:T(8,128)(2,1)} %pad_maximum_fusion.1), calls=%async_computation | async-start | bytes 2097152 | tf_op jit(solution)/shard_map/all_to_all | solution.py:164
  9.6 0.0 copy-done.3
  9.6 0.3 copy.20
  9.9 0.0 copy-done.4
  9.9 0.3 copy.21
  10.2 1.5 %pad_maximum_fusion = bf16[8,4,256,128]{3,2,1,0:T(8,128)(2,1)} fusion(bf16[8,2,256,128]{3,2,1,0:T(8,128)(2,1)S(1)} %bitcast.33, bf16[8,2,256,128]{3,2,1,0:T(8,128)(2,1)S(1)} %bitcast.32), kind=kLoop, calls=%fused_computation | loop fusion | flops 1048576 | bytes 4194304 | tf_op jit(solution)/shard_map/concatenate | solution.py:168
  11.7 0.0 copy-start.5
  11.7 13.7 %all-to-all-done.kv_ref = bf16[8,2,256,128]{3,2,1,0:T(8,128)(2,1)S(1)} async-done(((bf16[8,2,256,128]{3,2,1,0:T(8,128)(2,1)}), bf16[8,2,256,128]{3,2,1,0:T(8,128)(2,1)S(1)}, u32[]{:S(2)}, u32[]{:S(2)}) %all-to-all-start) | async-done | bytes 1048608 | tf_op jit(solution)/shard_map/all_to_all | solution.py:164
  25.4 3.6 %all-to-all-start.1 = ((bf16[8,4,256,128]{3,2,1,0:T(8,128)(2,1)}), bf16[8,4,256,128]{3,2,1,0:T(8,128)(2,1)S(1)}, u32[]{:S(2)}, u32[]{:S(2)}) async-start(bf16[8,4,256,128]{3,2,1,0:T(8,128)(2,1)} %pad_maximum_fusion), calls=%async_computation.1 | async-start | bytes 4194304 | tf_op jit(solution)/shard_map/all_to_all | solution.py:164
  29.0 0.0 copy-done.5
  29.1 0.1 select_reduce_fusion
  29.2 0.1 copy.22.ends_ref
  29.3 5.2 %collective-permute-start = (bf16[4,2,256,128]{3,2,1,0:T(8,128)(2,1)S(1)}, bf16[4,2,256,128]{3,2,1,0:T(8,128)(2,1)S(1)}, u32[]{:S(2)}, u32[]{:S(2)}) collective-permute-start(bf16[4,2,256,128]{3,2,1,0:T(8,128)(2,1)S(1)} %slice.29), channel_id=1, source_target_pairs={{0,16},{2,18},{4,20},{6,22},{8,24},{10,26},{12,28},{14,30},{1,17},... | collective-permute-start | bytes 1572872 | tf_op jit(solution)/shard_map/ppermute | solution.py:167
  34.6 0.2 select_reduce_fusion.1
  34.8 0.1 pad_add_fusion.meta_ref
  34.9 28.3 %collective-permute-done.halo_ref = bf16[4,2,256,128]{3,2,1,0:T(8,128)(2,1)S(1)} collective-permute-done((bf16[4,2,256,128]{3,2,1,0:T(8,128)(2,1)S(1)}, bf16[4,2,256,128]{3,2,1,0:T(8,128)(2,1)S(1)}, u32[]{:S(2)}, u32[]{:S(2)}) %collective-permute-start) | collective-permute-done | bytes 524320 | tf_op jit(solution)/shard_map/ppermute | solution.py:167
  63.1 0.0 copy-start.1
  63.1 0.8 copy-done.1
  63.9 0.0 all-to-all-done.1.x_ref
  63.9 0.0 copy-start.2
  63.9 1.0 copy-done.2
  64.9 13.1 %shard_map.84 = (bf16[8,4,256,128]{3,2,1,0:T(8,128)(2,1)S(1)}, f32[8,2,256,128]{3,2,1,0:T(8,128)S(1)}, bf16[4,2,256,128]{3,2,1,0:T(8,128)(2,1)S(1)}) custom-call(s32[9]{0:T(128)S(1)} %pad_add_fusion.meta_ref, s32[32,1]{1,0:T(8,128)S(1)} %copy.22.ends_ref, bf16[8,2,256,128]{3,2,1,0:T(8,128)(2,1)S(1)} %all-to-all-done.kv_ref, ...), custom_call_target="tpu_custom_call" | custom-call | flops 5000000000 | bytes 8388608 | tf_op jit(solution)/shard_map/pallas_call | solution.py:122
  78.1 0.0 copy-start
  78.1 1.3 collective-permute-start.1
  79.4 0.1 slice.39
  79.5 16.3 %collective-permute-done.1 = bf16[4,2,256,128]{3,2,1,0:T(8,128)(2,1)S(1)} collective-permute-done((bf16[4,2,256,128]{3,2,1,0:T(8,128)(2,1)S(1)}, bf16[4,2,256,128]{3,2,1,0:T(8,128)(2,1)S(1)}, u32[]{:S(2)}, u32[]{:S(2)}) %collective-permute-start.1) | collective-permute-done | bytes 524320 | tf_op jit(solution)/shard_map/ppermute | solution.py:173
  95.8 0.1 add_convert_fusion
  95.9 0.1 pad_maximum_fusion.2
  96.0 0.0 copy-done
  96.0 19.9 %all_to_all.20 = bf16[8,2,256,128]{3,2,1,0:T(8,128)(2,1)S(1)} all-to-all(bf16[8,2,256,128]{3,2,1,0:T(8,128)(2,1)S(1)} %pad_maximum_fusion.2), channel_id=1, replica_groups={{0,2,4,6,8,10,12,14},{16,18,20,22,24,26,28,30},{1,3,5,7,9,11,13,15},{17..., dimensions={0} | all-to-all | bytes 2097152 | tf_op jit(solution)/shard_map/all_to_all | solution.py:164
  115.9 3.8 %all-to-all-start.2 = ((bf16[8,4,256,128]{3,2,1,0:T(8,128)(2,1)}), bf16[8,4,256,128]{3,2,1,0:T(8,128)(2,1)S(1)}, u32[]{:S(2)}, u32[]{:S(2)}) async-start(bf16[8,4,256,128]{3,2,1,0:T(8,128)(2,1)} %copy-done), calls=%async_computation.2 | async-start | bytes 4194304 | tf_op jit(solution)/shard_map/all_to_all | solution.py:164
  119.7 0.1 slice_bitcast_fusion
  119.7 1.1 copy.26
  120.9 1.1 copy.25
  122.0 24.4 %all-to-all-done.2 = bf16[8,4,256,128]{3,2,1,0:T(8,128)(2,1)S(1)} async-done(((bf16[8,4,256,128]{3,2,1,0:T(8,128)(2,1)}), bf16[8,4,256,128]{3,2,1,0:T(8,128)(2,1)S(1)}, u32[]{:S(2)}, u32[]{:S(2)}) %all-to-all-start.2) | async-done | bytes 2097184 | tf_op jit(solution)/shard_map/all_to_all | solution.py:164
  146.4 0.1 fusion.1
  146.6 1.6 %copy.31 = bf16[16,256,128]{2,0,1:T(8,128)(2,1)} copy(bf16[16,256,128]{2,1,0:T(8,128)(2,1)S(1)} %bitcast.31) | data formatting | bytes 2097152 | tf_op jit(solution)/shard_map/reshape | solution.py:179
  148.3 1.6 %copy.32 = bf16[16,256,128]{2,0,1:T(8,128)(2,1)} copy(bf16[16,256,128]{2,1,0:T(8,128)(2,1)S(1)} %bitcast.30) | data formatting | bytes 2097152 | tf_op jit(solution)/shard_map/reshape | solution.py:178
  (3 shorter events, 0.1 us)
Async XLA Ops:
  2.0 7.6 %copy-start.3 = (bf16[256,16,128]{2,1,0:T(8,128)(2,1)S(1)}, bf16[256,16,128]{2,1,0:T(8,128)(2,1)}, u32[]{:S(2)}) copy-start(bf16[256,16,128]{2,1,0:T(8,128)(2,1)} %param.5) | copy-start | bytes 3145732
  3.1 6.8 %copy-start.4 = (bf16[256,16,128]{2,1,0:T(8,128)(2,1)S(1)}, bf16[256,16,128]{2,1,0:T(8,128)(2,1)}, u32[]{:S(2)}) copy-start(bf16[256,16,128]{2,1,0:T(8,128)(2,1)} %param.8) | copy-start | bytes 3145732
  3.1 22.3 %all-to-all-start = ((bf16[8,2,256,128]{3,2,1,0:T(8,128)(2,1)}), bf16[8,2,256,128]{3,2,1,0:T(8,128)(2,1)S(1)}, u32[]{:S(2)}, u32[]{:S(2)}) async-start(bf16[8,2,256,128]{3,2,1,0:T(8,128)(2,1)} %pad_maximum_fusion.1), calls=%async_computation | async-start | bytes 2097152 | tf_op jit(solution)/shard_map/all_to_all | solution.py:164
  11.7 17.4 %copy-start.5 = (s32[32]{0:T(128)S(1)}, s32[32]{0:T(128)}, u32[]{:S(2)}) copy-start(s32[32]{0:T(128)} %param.9) | copy-start | bytes 388
  25.4 38.5 %all-to-all-start.1 = ((bf16[8,4,256,128]{3,2,1,0:T(8,128)(2,1)}), bf16[8,4,256,128]{3,2,1,0:T(8,128)(2,1)S(1)}, u32[]{:S(2)}, u32[]{:S(2)}) async-start(bf16[8,4,256,128]{3,2,1,0:T(8,128)(2,1)} %pad_maximum_fusion), calls=%async_computation.1 | async-start | bytes 4194304 | tf_op jit(solution)/shard_map/all_to_all | solution.py:164
  29.3 33.8 %collective-permute-start = (bf16[4,2,256,128]{3,2,1,0:T(8,128)(2,1)S(1)}, bf16[4,2,256,128]{3,2,1,0:T(8,128)(2,1)S(1)}, u32[]{:S(2)}, u32[]{:S(2)}) collective-permute-start(bf16[4,2,256,128]{3,2,1,0:T(8,128)(2,1)S(1)} %slice.29), channel_id=1, source_target_pairs={{0,16},{2,18},{4,20},{6,22},{8,24},{10,26},{12,28},{14,30},{1,17},... | collective-permute-start | bytes 1572872 | tf_op jit(solution)/shard_map/ppermute | solution.py:167
  63.1 0.8 copy-start.1
  63.9 1.0 copy-start.2
  78.1 17.9 %copy-start = (bf16[8,4,256,128]{3,2,1,0:T(8,128)(2,1)}, bf16[8,4,256,128]{3,2,1,0:T(8,128)(2,1)S(1)}, u32[]{:S(2)}) copy-start(bf16[8,4,256,128]{3,2,1,0:T(8,128)(2,1)S(1)} %get-tuple-element.7) | copy-start | bytes 6291460
  78.1 17.7 %collective-permute-start.1 = (bf16[4,2,256,128]{3,2,1,0:T(8,128)(2,1)S(1)}, bf16[4,2,256,128]{3,2,1,0:T(8,128)(2,1)S(1)}, u32[]{:S(2)}, u32[]{:S(2)}) collective-permute-start(bf16[4,2,256,128]{3,2,1,0:T(8,128)(2,1)S(1)} %get-tuple-element.9), channel_id=1, source_target_pairs={{16,0},{18,2},{20,4},{22,6},{24,8},{26,10},{28,12},{30,14},{17,1},... | collective-permute-start | bytes 1572872 | tf_op jit(solution)/shard_map/ppermute | solution.py:173
  115.9 30.6 %all-to-all-start.2 = ((bf16[8,4,256,128]{3,2,1,0:T(8,128)(2,1)}), bf16[8,4,256,128]{3,2,1,0:T(8,128)(2,1)S(1)}, u32[]{:S(2)}, u32[]{:S(2)}) async-start(bf16[8,4,256,128]{3,2,1,0:T(8,128)(2,1)} %copy-done), calls=%async_computation.2 | async-start | bytes 4194304 | tf_op jit(solution)/shard_map/all_to_all | solution.py:164

commit v2 on v1

v2 whole, which is shorter than its diff:
```python
import functools

import jax
import jax.numpy as jnp
from jax import lax
from jax.experimental import pallas as pl
from jax.experimental.pallas import tpu as pltpu
from jax.sharding import PartitionSpec as P

WINDOW = 1024
SCALING = 168.0 ** (-0.5)
LOG2E = 1.4426950408889634
NEG = -1e30
PIECES = 2

NT = (((1,), (1,)), ((), ()))
NN = (((1,), (0,)), ((), ()))

VMEM = pl.BlockSpec(memory_space=pltpu.VMEM)
SMEM = pl.BlockSpec(memory_space=pltpu.SMEM)


def dot(a, b, dims):
    return lax.dot_general(a, b, dims, preferred_element_type=jnp.float32)


def place(i, turn, blocks):
    return lax.rem(i + turn, blocks)


def prepare_kernel(meta_ref, kv_ref, halo_ref, k_ref, kt_ref, *, blocks, tile):
    before = halo_ref.shape[0]
    cuts = kv_ref.shape[2] // tile
    turn = meta_ref[blocks + 1]

    def put(source, index, at):
        for n in range(2):
            for c in range(cuts):
                part = source[index, n, c * tile:(c + 1) * tile]
                k_ref[at * cuts + c, n] = part
                kt_ref[at * cuts + c, n] = part.T

    def halo_step(t, carry):
        put(halo_ref, t, t)
        return carry

    def own_step(t, carry):
        put(kv_ref, place(t, turn, blocks), before + t)
        return carry

    lax.fori_loop(0, before, halo_step, 0)
    lax.fori_loop(0, blocks, own_step, 0, unroll=2)


def prepare(meta, kv, halo, tile):
    blocks, _, rows, dim = kv.shape
    tiles = (halo.shape[0] + blocks) * (rows // tile)
    return pl.pallas_call(
        functools.partial(prepare_kernel, blocks=blocks, tile=tile),
        out_shape=(
            jax.ShapeDtypeStruct((tiles, 2, tile, dim), kv.dtype),
            jax.ShapeDtypeStruct((tiles, 2, dim, tile), kv.dtype),
        ),
        in_specs=[SMEM, VMEM, VMEM],
        out_specs=(VMEM, VMEM),
        compiler_params=pltpu.CompilerParams(vmem_limit_bytes=12 * 1024 * 1024),
        cost_estimate=pl.CostEstimate(flops=10**6, bytes_accessed=6 * 2**20, transcendentals=0),
    )(meta, kv, halo)


def attention_kernel(*refs, blocks, before, group, piece, first_piece, last_piece):
    refs = list(refs)
    meta_ref, ends_ref, k_ref, kt_ref, x_ref = refs[:5]
    refs = refs[5:]
    if not first_piece:
        given_ref = refs.pop(0)
    y_ref = refs.pop(0)
    if last_piece:
        dkv_ref, dhalo_ref, acc_ref, s_ref, g_ref = refs
    else:
        acc_ref, s_ref, g_ref = refs
    tile, dim = x_ref.shape[2:]
    wide = group * tile
    tiles = k_ref.shape[0]
    cuts = tiles // (blocks + before)
    base, turn = meta_ref[blocks], meta_ref[blocks + 1]

    def start_step(t, carry):
        if first_piece:
            acc_ref[t] = jnp.zeros(acc_ref.shape[1:], jnp.float32)
        else:
            acc_ref[t] = given_ref[t]
        return carry

    lax.fori_loop(0, tiles, start_step, 0, unroll=4)

    lane = lax.rem(lax.broadcasted_iota(jnp.int32, (1, wide), 1), tile)
    diff = lane - lax.broadcasted_iota(jnp.int32, (2 * tile, wide), 0)

    def query_tile(i, count):
        own = (i + before) * cuts + piece
        first = own - (count - 1)
        at = place(i, turn, blocks)
        q = x_ref[at, 0:group].reshape(wide, dim)
        do = x_ref[at, group:2 * group].reshape(wide, dim)
        pos = base + (i * cuts + piece) * tile + lane
        ends = ends_ref[...]
        start = jnp.max(jnp.where(ends <= pos, ends, 0), axis=0, keepdims=True)
        reach = pos - jnp.maximum(start, pos - (WINDOW - 1))
        chunks = [(0, 1)] * (count % 2) + [(a, 2) for a in range(count % 2, count, 2)]
        top = None
        for a, n in chunks:
            raw = dot(k_ref[pl.ds(first + a, n), 0].reshape(n * tile, dim), q, NT)
            offset = (count - 1 - a) * tile
            keep = diff[:n * tile] <= reach - offset
            if a + n == count:
                keep = keep & (diff[:n * tile] >= -offset)
            raw = jnp.where(keep, raw, NEG)
            s_ref[a * tile:(a + n) * tile] = raw
            here = jnp.max(raw, axis=0, keepdims=True)
            top = here if top is None else jnp.maximum(top, here)
            g_ref[a * tile:(a + n) * tile] = dot(k_ref[pl.ds(first + a, n), 1].reshape(n * tile, dim), do, NT)
        total = mixed = 0.0
        for a, n in chunks:
            p = jnp.exp2((s_ref[a * tile:(a + n) * tile] - top) * (SCALING * LOG2E))
            s_ref[a * tile:(a + n) * tile] = p
            total += jnp.sum(p, axis=0, keepdims=True)
            mixed += jnp.sum(p * g_ref[a * tile:(a + n) * tile], axis=0, keepdims=True)
        inverse = 1.0 / total
        row_total = mixed * inverse
        out = dq = 0.0
        for a, n in chunks:
            w = s_ref[a * tile:(a + n) * tile] * inverse
            wb = w.astype(jnp.bfloat16)
            ds = (w * (g_ref[a * tile:(a + n) * tile] - row_total)).astype(jnp.bfloat16)
            kt, vt = (
                jnp.concatenate([kt_ref[first + a + c, m] for c in range(n)], axis=1) for m in range(2)
            )
            out += dot(vt, wb, NN)
            dq += dot(kt, ds, NN)
            acc_ref[pl.ds(first + a, n), 1] += dot(wb, do, NN).reshape(n, tile, dim)
            acc_ref[pl.ds(first + a, n), 0] += dot(ds, q, NN).reshape(n, tile, dim)
        for n in range(group):
            y_ref[at, n] = out[:, n * tile:(n + 1) * tile].T.astype(jnp.bfloat16)
            y_ref[at, group + n] = (SCALING * dq[:, n * tile:(n + 1) * tile]).T.astype(jnp.bfloat16)

    def query_step(i, carry):
        count = meta_ref[i]
        for n in range(1, before * cuts + 2):
            pl.when(count == n)(functools.partial(query_tile, i, n))
        return carry

    lax.fori_loop(0, blocks, query_step, 0)

    if last_piece:
        def result(t, c):
            return SCALING * acc_ref[t * cuts + c, 0], acc_ref[t * cuts + c, 1]

        def halo_step(t, carry):
            for c in range(cuts):
                for n, value in enumerate(result(t, c)):
                    dhalo_ref[t, n * cuts + c] = value.astype(jnp.bfloat16)
            return carry

        def own_step(t, carry):
            for c in range(cuts):
                for n, value in enumerate(result(before + t, c)):
                    dkv_ref[place(t, turn, blocks), n * cuts + c] = value
            return carry

        lax.fori_loop(0, before, halo_step, 0)
        lax.fori_loop(0, blocks, own_step, 0, unroll=2)


def attention(meta, ends, k, kt, x, given, before, piece):
    blocks, _, tile, dim = x.shape
    group = x.shape[1] // 2
    tiles = k.shape[0]
    cuts = tiles // (blocks + before)
    first_piece, last_piece = given is None, piece == PIECES - 1
    acc = jax.ShapeDtypeStruct((tiles, 2, tile, dim), jnp.float32)
    outs = [jax.ShapeDtypeStruct(x.shape, jnp.bfloat16)]
    scratch = [pltpu.VMEM(((before * cuts + 1) * tile, group * tile), jnp.float32)] * 2
    if last_piece:
        outs += [
            jax.ShapeDtypeStruct((blocks, 2 * cuts, tile, dim), jnp.float32),
            jax.ShapeDtypeStruct((before, 2 * cuts, tile, dim), jnp.bfloat16),
        ]
        scratch = [pltpu.VMEM(acc.shape, acc.dtype)] + scratch
    else:
        outs.append(acc)
    operands = [meta, ends, k, kt, x] + ([] if first_piece else [given])
    return pl.pallas_call(
        functools.partial(
            attention_kernel, blocks=blocks, before=before, group=group, piece=piece,
            first_piece=first_piece, last_piece=last_piece,
        ),
        out_shape=tuple(outs),
        in_specs=[SMEM] + [VMEM] * (len(operands) - 1),
        out_specs=(VMEM,) * len(outs),
        scratch_shapes=scratch,
        compiler_params=pltpu.CompilerParams(vmem_limit_bytes=20 * 1024 * 1024),
        cost_estimate=pl.CostEstimate(flops=3 * 10**9, bytes_accessed=12 * 2**20, transcendentals=2 * 10**6),
    )(*operands)


def after(array, other):
    return lax.optimization_barrier((array, other))[0]


def body(queries, keys, values, out_grad, doc_lengths):
    rows, heads, dim = queries.shape
    kv_heads = keys.shape[1]
    group = heads // kv_heads
    blocks = kv_heads
    parts = lax.axis_size("ctx") // blocks
    before = WINDOW // rows
    tile = rows // PIECES
    turns = [(p % 2) * (blocks // 2) for p in range(parts)]
    groups = [[p * blocks + (r + turns[p]) % blocks for r in range(blocks)] for p in range(parts)]
    onward = [(groups[p][r], groups[p + 1][r]) for p in range(parts - 1) for r in range(blocks)]
    part = lax.axis_index("ctx") // blocks

    docs = doc_lengths.shape[0]
    upto = jnp.arange(docs)[:, None] >= jnp.arange(docs)[None, :]
    ends = jnp.sum(jnp.where(upto, doc_lengths[None, :], 0), axis=1)
    base = part * blocks * rows
    turn = lax.rem(part, 2) * (blocks // 2)
    metas = []
    for piece in range(PIECES):
        position = base + jnp.arange(blocks, dtype=jnp.int32) * rows + piece * tile
        start = jnp.max(jnp.where(ends[None, :] <= position[:, None], ends[None, :], 0), axis=1)
        first = jnp.maximum(jnp.maximum(start, position - (WINDOW - 1)), 0)
        metas.append(jnp.concatenate((position // tile - first // tile + 1, jnp.stack((base, turn)))).astype(jnp.int32))
    ends = ends[:, None].astype(jnp.int32)

    def exchange(array):
        return lax.all_to_all(array, "ctx", 0, 0, axis_index_groups=groups)

    def by_head(array):
        array = jnp.swapaxes(array, 0, 1)
        return array.reshape(kv_heads, array.shape[0] // kv_heads, array.shape[1], dim)

    def by_token(array):
        array = array.reshape(array.shape[0] * array.shape[1], array.shape[2], dim)
        return jnp.swapaxes(array, 0, 1)

    kv = exchange(jnp.concatenate((by_head(keys), by_head(values)), 1))
    tail = jnp.stack([kv[(blocks - before + t + turns[0]) % blocks] for t in range(before)]) if turns[0] else kv[blocks - before:]
    halo = lax.ppermute(tail, "ctx", onward)
    packed = [
        jnp.concatenate([by_head(a[p * tile:(p + 1) * tile]) for a in (queries, out_grad)], 1) for p in range(PIECES)
    ]
    x0 = exchange(after(packed[0], kv))
    k, kt = prepare(metas[0], kv, halo, tile)
    x1 = exchange(after(packed[1], x0))
    y0, acc = attention(metas[0], ends, k, kt, x0, None, before, 0)
    y1, dkv, dhalo = attention(metas[1], ends, k, kt, x1, acc, before, 1)
    dhalo = lax.ppermute(dhalo, "ctx", [(b, a) for a, b in onward])
    y0 = exchange(after(y0, x1))
    still = blocks - before
    dkv = jnp.concatenate((dkv[:still], dkv[still:] + dhalo.astype(jnp.float32)), 0).astype(jnp.bfloat16)
    last = exchange(after(jnp.concatenate((y1, dkv), 1), y0))
    y1, dk, dv = last[:, :2 * group], last[:, 2 * group:2 * group + PIECES], last[:, 2 * group + PIECES:]
    attended = jnp.concatenate([by_token(y[:, :group]) for y in (y0, y1)], 0)
    query_grad = jnp.concatenate([by_token(y[:, group:]) for y in (y0, y1)], 0)
    dk, dv = (jnp.swapaxes(a.reshape(kv_heads, rows, dim), 0, 1) for a in (dk, dv))
    return attended, query_grad, dk, dv


def solution(mesh):
    spec = P(("dp", "ctx"), "head", None)
    return jax.shard_map(
        body,
        mesh=mesh,
        in_specs=(spec, spec, spec, spec, P("dp")),
        out_specs=(spec, spec, spec, spec),
        check_vma=False,
    )
```

time: 152 us -> 138 us (0.908)
  waiting for transfers between devices: 82.7 us -> 58.9 us
  blocking collectives: 19.9 us -> 0 us
  local copies, waits for them, and re-layouts: 9.78 us -> 20 us
  starting transfers between devices: 20.4 us -> 27.9 us
  other arithmetic: 3.18 us -> 9.59 us
  Pallas kernels: 13.1 us -> 18.5 us
    ppermute x1, waiting for transfers between devices: 28.3 us -> 0.01 us  [body(): halo = lax.ppermute(tail, 'ctx', onward)]
    all_to_all x1 -> x0, blocking collectives: 19.9 us -> none  [exchange(): return lax.all_to_all(array, 'ctx', 0, 0, axis_index_groups=groups)]
    all_to_all x3 -> x5, waiting for transfers between devices: 38.2 us -> 48.7 us  [exchange(): return lax.all_to_all(array, 'ctx', 0, 0, axis_index_groups=groups)]
    all_to_all x3 -> x5, starting transfers between devices: 13.9 us -> 21.5 us  [exchange(): return lax.all_to_all(array, 'ctx', 0, 0, axis_index_groups=groups)]
    unnamed x14 -> x22, local copies, waits for them, and re-layouts: 4.12 us -> 10.6 us
    concatenate x3 -> x8, other arithmetic: 1.69 us -> 8.06 us  [the longest x2 3.17 us: body(): jnp.concatenate([by_head(a[p * tile:(p + 1) * tile]) for a in (queries, o...]
    ppermute x1, waiting for transfers between devices: 16.3 us -> 10.2 us  [body(): dhalo = lax.ppermute(dhalo, 'ctx', [(b, a) for a, b in onward])]
    pallas_call x1 -> x3, Pallas kernels: 13.1 us -> 18.5 us  [the longest x2 16.5 us: attention(): pl.pallas_call(functools.partial(attention_kernel, blocks=blocks, before=...]
  transfers between devices with their start and end apart: 5 -> 7, of which waited for: 4 -> 6; matrix products, arithmetic and copies ran while one was open for 3% -> 8% of each run, Pallas kernels for 0% -> 7%
where the time goes in v2:
time: 138 us; the launch traced here: 136 us
  waiting for transfers between devices  58.9 us (43%)
  starting transfers between devices  27.9 us (20%)
  local copies, waits for them, and re-layouts  20 us (14%)
  Pallas kernels  18.5 us (13%)
  other arithmetic  9.59 us (7%)
    all_to_all x5, waiting for transfers between devices, exchange(): return lax.all_to_all(array, 'ctx', 0, 0, axis_index_groups=groups)  48.7 us
    all_to_all x5, starting transfers between devices, exchange(): return lax.all_to_all(array, 'ctx', 0, 0, axis_index_groups=groups)  21.5 us
    pallas_call x2, Pallas kernels, attention(): pl.pallas_call(functools.partial(attention_kernel, blocks=blocks, before=...  16.5 us
    unnamed x22, local copies, waits for them, and re-layouts  10.6 us
    ppermute x1, waiting for transfers between devices, body(): dhalo = lax.ppermute(dhalo, 'ctx', [(b, a) for a, b in onward])  10.2 us
    ppermute x1, starting transfers between devices, body(): halo = lax.ppermute(tail, 'ctx', onward)  5.11 us
    concatenate x2, other arithmetic, body(): jnp.concatenate([by_head(a[p * tile:(p + 1) * tile]) for a in (queries, o...  3.17 us
    transpose x6, local copies, waits for them, and re-layouts, by_head(): array = jnp.swapaxes(array, 0, 1)  2.99 us
  transfers between devices with their start and end apart: 7, of which 6 were waited for; matrix products, arithmetic and copies ran while one was open for 8% of the time, Pallas kernels for 7%

profile of v2, /device:TPU:1, one launch (start us, length us, event | category | flops | bytes accessed | tf_op | source)
XLA Modules:
  0.0 135.7 jit_solution(7405871289994975765)
XLA Ops:
  0.6 1.4 %copy_bitcast_fusion.6 = (bf16[8,1,256,128]{3,2,1,0:T(8,128)(2,1)S(1)}, bf16[8,1,256,128]{3,2,1,0:T(8,128)(2,1)S(1)}) fusion(bf16[256,8,128]{2,1,0:T(8,128)(2,1)} %param.7, bf16[256,8,128]{2,1,0:T(8,128)(2,1)} %param.6), kind=kLoop, calls=%fused_computation.14 | loop fusion | bytes 2097152 | tf_op jit(solution)/shard_map/reshape | solution.py:242
  2.0 1.1 pad_maximum_fusion
  3.1 6.4 %all-to-all-start = ((bf16[8,2,256,128]{3,2,1,0:T(8,128)(2,1)}), bf16[8,2,256,128]{3,2,1,0:T(8,128)(2,1)S(1)}, u32[]{:S(2)}, u32[]{:S(2)}) async-start(bf16[8,2,256,128]{3,2,1,0:T(8,128)(2,1)} %pad_maximum_fusion), calls=%async_computation | async-start | bytes 2097152 | tf_op jit(solution)/shard_map/all_to_all | solution.py:238
  9.5 1.5 %slice_bitcast_fusion.3 = (bf16[16,128,128]{2,0,1:T(8,128)(2,1)S(1)}, bf16[16,128,128]{2,0,1:T(8,128)(2,1)S(1)}) fusion(bf16[256,16,128]{2,1,0:T(8,128)(2,1)} %param.5), kind=kLoop, calls=%fused_computation.19 | loop fusion | bytes 2097152 | tf_op jit(solution)/shard_map/transpose | solution.py:241
  10.9 0.1 copy.25
  11.1 0.2 slice_bitcast_fusion.2
  11.3 0.1 copy.26
  11.4 1.1 pad_maximum_fusion.1
  12.5 12.8 %all-to-all-done.kv_ref = bf16[8,2,256,128]{3,2,1,0:T(8,128)(2,1)S(1)} async-done(((bf16[8,2,256,128]{3,2,1,0:T(8,128)(2,1)}), bf16[8,2,256,128]{3,2,1,0:T(8,128)(2,1)S(1)}, u32[]{:S(2)}, u32[]{:S(2)}) %all-to-all-start) | async-done | bytes 1048608 | tf_op jit(solution)/shard_map/all_to_all | solution.py:238
  25.3 3.6 %all-to-all-start.1 = ((bf16[8,4,128,128]{3,2,1,0:T(8,128)(2,1)}), bf16[8,4,128,128]{3,2,1,0:T(8,128)(2,1)S(1)}, u32[]{:S(2)}, u32[]{:S(2)}) async-start(bf16[8,4,128,128]{3,2,1,0:T(8,128)(2,1)} %pad_maximum_fusion.1), calls=%async_computation.1 | async-start | bytes 2097152 | tf_op jit(solution)/shard_map/all_to_all | solution.py:238
  28.9 0.9 copy.28
  29.8 0.1 copy.29
  30.0 0.1 select_reduce_fusion
  30.1 0.2 select_reduce_fusion.2
  30.3 2.1 %pad_maximum_fusion.2 = bf16[8,4,128,128]{3,2,1,0:T(8,128)(2,1)} fusion(bf16[8,2,128,128]{3,2,1,0:T(8,128)(2,1)S(1)} %bitcast.48, bf16[8,2,128,128]{3,2,1,0:T(8,128)(2,1)} %bitcast.47), kind=kLoop, calls=%fused_computation.4 | loop fusion | flops 524288 | bytes 2097152 | tf_op jit(solution)/shard_map/concatenate | solution.py:252
  32.4 0.8 slice.56
  33.2 5.1 %collective-permute-start = (bf16[4,2,256,128]{3,2,1,0:T(8,128)(2,1)}, bf16[4,2,256,128]{3,2,1,0:T(8,128)(2,1)}, u32[]{:S(2)}, u32[]{:S(2)}) collective-permute-start(bf16[4,2,256,128]{3,2,1,0:T(8,128)(2,1)} %slice.56), channel_id=1, source_target_pairs={{0,24},{2,26},{4,28},{6,30},{8,16},{10,18},{12,20},{14,22},{1,25},... | collective-permute-start | bytes 1572872 | tf_op jit(solution)/shard_map/ppermute | solution.py:250
  38.4 6.3 %all-to-all-done.1.refs_4_ = bf16[8,4,128,128]{3,2,1,0:T(8,128)(2,1)S(1)} async-done(((bf16[8,4,128,128]{3,2,1,0:T(8,128)(2,1)}), bf16[8,4,128,128]{3,2,1,0:T(8,128)(2,1)S(1)}, u32[]{:S(2)}, u32[]{:S(2)}) %all-to-all-start.1) | async-done | bytes 1048608 | tf_op jit(solution)/shard_map/all_to_all | solution.py:238
  44.6 3.6 %all-to-all-start.2 = ((bf16[8,4,128,128]{3,2,1,0:T(8,128)(2,1)}), bf16[8,4,128,128]{3,2,1,0:T(8,128)(2,1)S(1)}, u32[]{:S(2)}, u32[]{:S(2)}) async-start(bf16[8,4,128,128]{3,2,1,0:T(8,128)(2,1)} %pad_maximum_fusion.2), calls=%async_computation.2 | async-start | bytes 2097152 | tf_op jit(solution)/shard_map/all_to_all | solution.py:238
  48.5 2.0 %shard_map.84 = (bf16[24,2,128,128]{3,2,1,0:T(8,128)(2,1)S(1)}, bf16[24,2,128,128]{3,2,1,0:T(8,128)(2,1)S(1)}) custom-call(s32[10]{0:T(128)S(1)} %add_add_fusion.meta_ref.refs_0_, bf16[8,2,256,128]{3,2,1,0:T(8,128)(2,1)S(1)} %all-to-all-done.kv_ref, bf16[4,2,256,128]{3,2,1,0:T(8,128)(2,1)} %collective-permute-done.halo_ref), custom_call_target="tpu_custom_call" | custom-call | flops 1000000 | bytes 6291456 | tf_op jit(solution)/shard_map/pallas_call | solution.py:58
  50.5 7.9 %shard_map.85 = (bf16[8,4,128,128]{3,2,1,0:T(8,128)(2,1)S(1)}, f32[24,2,128,128]{3,2,1,0:T(8,128)S(1)}) custom-call(s32[10]{0:T(128)S(1)} %add_add_fusion.meta_ref.refs_0_, s32[32,1]{1,0:T(8,128)S(1)} %copy.27.refs_1_, bf16[24,2,128,128]{3,2,1,0:T(8,128)(2,1)S(1)} %get-tuple-element.15.refs_2_, bf16[24,2,128,128]{3,2,1,0:T(8,128)(2,1)S(1)} %get-tuple-element.16.refs_3_, ...), custom_call_target="tpu_custom_call" | custom-call | flops 3000000000 | bytes 12582912 | tf_op jit(solution)/shard_map/pallas_call | solution.py:193
  58.4 1.0 copy-done
  59.3 1.2 copy-done.3
  60.5 1.2 copy-done.5
  61.7 1.6 %copy-done.7 = f32[24,2,128,128]{3,2,1,0:T(8,128)} copy-done((f32[24,2,128,128]{3,2,1,0:T(8,128)}, f32[24,2,128,128]{3,2,1,0:T(8,128)S(1)}, u32[]{:S(2)}) %copy-start.7) | copy-done | bytes 3145752
  63.3 0.7 all-to-all-done.2.refs_4_
  64.0 1.4 %copy-done.4 = bf16[24,2,128,128]{3,2,1,0:T(8,128)(2,1)S(1)} copy-done((bf16[24,2,128,128]{3,2,1,0:T(8,128)(2,1)S(1)}, bf16[24,2,128,128]{3,2,1,0:T(8,128)(2,1)}, u32[]{:S(2)}) %copy-start.4) | copy-done | bytes 1572888
  65.4 1.4 %copy-done.6 = bf16[24,2,128,128]{3,2,1,0:T(8,128)(2,1)S(1)} copy-done((bf16[24,2,128,128]{3,2,1,0:T(8,128)(2,1)S(1)}, bf16[24,2,128,128]{3,2,1,0:T(8,128)(2,1)}, u32[]{:S(2)}) %copy-start.6) | copy-done | bytes 1572888
  66.8 1.9 %copy-done.8 = f32[24,2,128,128]{3,2,1,0:T(8,128)S(1)} copy-done((f32[24,2,128,128]{3,2,1,0:T(8,128)S(1)}, f32[24,2,128,128]{3,2,1,0:T(8,128)}, u32[]{:S(2)}) %copy-start.8) | copy-done | bytes 3145752
  68.7 8.6 %shard_map.86 = (bf16[8,4,128,128]{3,2,1,0:T(8,128)(2,1)S(1)}, f32[8,4,128,128]{3,2,1,0:T(8,128)S(1)}, bf16[4,4,128,128]{3,2,1,0:T(8,128)(2,1)}) custom-call(s32[10]{0:T(128)S(1)} %add_add_fusion.1.refs_0_, s32[32,1]{1,0:T(8,128)S(1)} %copy.27.refs_1_, bf16[24,2,128,128]{3,2,1,0:T(8,128)(2,1)S(1)} %copy-done.4, bf16[24,2,128,128]{3,2,1,0:T(8,128)(2,1)S(1)} %copy-done.6, ...), custom_call_target="tpu_custom_call" | custom-call | flops 3000000000 | bytes 12582912 | tf_op jit(solution)/shard_map/pallas_call | solution.py:193
  77.3 1.0 copy-done.1
  78.3 1.3 collective-permute-start.1
  79.5 4.4 %all-to-all-start.3 = ((bf16[8,4,128,128]{3,2,1,0:T(8,128)(2,1)}), bf16[8,4,128,128]{3,2,1,0:T(8,128)(2,1)S(1)}, u32[]{:S(2)}, u32[]{:S(2)}) async-start(bf16[8,4,128,128]{3,2,1,0:T(8,128)(2,1)} %copy-done), calls=%async_computation.3 | async-start | bytes 2097152 | tf_op jit(solution)/shard_map/all_to_all | solution.py:238
  84.1 10.2 %collective-permute-done.1 = bf16[4,4,128,128]{3,2,1,0:T(8,128)(2,1)} collective-permute-done((bf16[4,4,128,128]{3,2,1,0:T(8,128)(2,1)}, bf16[4,4,128,128]{3,2,1,0:T(8,128)(2,1)}, u32[]{:S(2)}, u32[]{:S(2)}) %collective-permute-start.1) | collective-permute-done | bytes 524320 | tf_op jit(solution)/shard_map/ppermute | solution.py:259
  94.2 1.2 add_convert_fusion
  95.4 1.5 %maximum_maximum_fusion = bf16[8,8,128,128]{3,2,1,0:T(8,128)(2,1)} fusion(bf16[4,4,128,128]{3,2,1,0:T(8,128)(2,1)S(1)} %add_convert_fusion, bf16[4,4,128,128]{3,2,1,0:T(8,128)(2,1)S(1)} %slice.70, bf16[8,4,128,128]{3,2,1,0:T(8,128)(2,1)S(1)} %copy-done.2), kind=kLoop, calls=%fused_computation | loop fusion | flops 2097152 | bytes 4194304 | tf_op jit(solution)/shard_map/concatenate | solution.py:263
  97.0 2.8 %all-to-all-done.3 = bf16[8,4,128,128]{3,2,1,0:T(8,128)(2,1)S(1)} async-done(((bf16[8,4,128,128]{3,2,1,0:T(8,128)(2,1)}), bf16[8,4,128,128]{3,2,1,0:T(8,128)(2,1)S(1)}, u32[]{:S(2)}, u32[]{:S(2)}) %all-to-all-start.3) | async-done | bytes 1048608 | tf_op jit(solution)/shard_map/all_to_all | solution.py:238
  99.8 3.6 %all-to-all-start.4 = ((bf16[8,8,128,128]{3,2,1,0:T(8,128)(2,1)}), bf16[8,8,128,128]{3,2,1,0:T(8,128)(2,1)S(1)}, u32[]{:S(2)}, u32[]{:S(2)}) async-start(bf16[8,8,128,128]{3,2,1,0:T(8,128)(2,1)} %maximum_maximum_fusion), calls=%async_computation.4 | async-start | bytes 4194304 | tf_op jit(solution)/shard_map/all_to_all | solution.py:238
  103.5 0.3 copy.48
  103.8 0.3 copy.50
  104.2 26.2 %all-to-all-done.4 = bf16[8,8,128,128]{3,2,1,0:T(8,128)(2,1)S(1)} async-done(((bf16[8,8,128,128]{3,2,1,0:T(8,128)(2,1)}), bf16[8,8,128,128]{3,2,1,0:T(8,128)(2,1)S(1)}, u32[]{:S(2)}, u32[]{:S(2)}) %all-to-all-start.4) | async-done | bytes 2097184 | tf_op jit(solution)/shard_map/all_to_all | solution.py:238
  130.4 0.2 fusion
  130.6 1.1 copy.45
  131.8 1.1 copy.46
  132.9 0.3 copy.47
  133.2 0.3 copy.49
  133.6 1.1 pad_maximum_fusion.4
  134.7 1.1 pad_maximum_fusion.3
  (23 shorter events, 0.5 us)
Async XLA Ops:
  3.1 22.2 %all-to-all-start = ((bf16[8,2,256,128]{3,2,1,0:T(8,128)(2,1)}), bf16[8,2,256,128]{3,2,1,0:T(8,128)(2,1)S(1)}, u32[]{:S(2)}, u32[]{:S(2)}) async-start(bf16[8,2,256,128]{3,2,1,0:T(8,128)(2,1)} %pad_maximum_fusion), calls=%async_computation | async-start | bytes 2097152 | tf_op jit(solution)/shard_map/all_to_all | solution.py:238
  9.5 1.6 %copy-start.9 = (bf16[256,16,128]{2,1,0:T(8,128)(2,1)S(1)}, bf16[256,16,128]{2,1,0:T(8,128)(2,1)}, u32[]{:S(2)}) copy-start(bf16[256,16,128]{2,1,0:T(8,128)(2,1)} %param.8) | copy-start | bytes 3145732
  12.5 17.5 %copy-start.10 = (s32[32]{0:T(128)S(1)}, s32[32]{0:T(128)}, u32[]{:S(2)}) copy-start(s32[32]{0:T(128)} %param.9) | copy-start | bytes 388
  25.3 19.3 %all-to-all-start.1 = ((bf16[8,4,128,128]{3,2,1,0:T(8,128)(2,1)}), bf16[8,4,128,128]{3,2,1,0:T(8,128)(2,1)S(1)}, u32[]{:S(2)}, u32[]{:S(2)}) async-start(bf16[8,4,128,128]{3,2,1,0:T(8,128)(2,1)} %pad_maximum_fusion.1), calls=%async_computation.1 | async-start | bytes 2097152 | tf_op jit(solution)/shard_map/all_to_all | solution.py:238
  33.2 15.2 %collective-permute-start = (bf16[4,2,256,128]{3,2,1,0:T(8,128)(2,1)}, bf16[4,2,256,128]{3,2,1,0:T(8,128)(2,1)}, u32[]{:S(2)}, u32[]{:S(2)}) collective-permute-start(bf16[4,2,256,128]{3,2,1,0:T(8,128)(2,1)} %slice.56), channel_id=1, source_target_pairs={{0,24},{2,26},{4,28},{6,30},{8,16},{10,18},{12,20},{14,22},{1,25},... | collective-permute-start | bytes 1572872 | tf_op jit(solution)/shard_map/ppermute | solution.py:250
  44.6 19.3 %all-to-all-start.2 = ((bf16[8,4,128,128]{3,2,1,0:T(8,128)(2,1)}), bf16[8,4,128,128]{3,2,1,0:T(8,128)(2,1)S(1)}, u32[]{:S(2)}, u32[]{:S(2)}) async-start(bf16[8,4,128,128]{3,2,1,0:T(8,128)(2,1)} %pad_maximum_fusion.2), calls=%async_computation.2 | async-start | bytes 2097152 | tf_op jit(solution)/shard_map/all_to_all | solution.py:238
  58.3 1.0 copy-start
  59.3 1.2 copy-start.3
  60.5 1.2 copy-start.5
  61.7 1.6 %copy-start.7 = (f32[24,2,128,128]{3,2,1,0:T(8,128)}, f32[24,2,128,128]{3,2,1,0:T(8,128)S(1)}, u32[]{:S(2)}) copy-start(f32[24,2,128,128]{3,2,1,0:T(8,128)S(1)} %get-tuple-element.21.refs_5_) | copy-start | bytes 9437188
  64.0 1.4 %copy-start.4 = (bf16[24,2,128,128]{3,2,1,0:T(8,128)(2,1)S(1)}, bf16[24,2,128,128]{3,2,1,0:T(8,128)(2,1)}, u32[]{:S(2)}) copy-start(bf16[24,2,128,128]{3,2,1,0:T(8,128)(2,1)} %copy-done.3) | copy-start | bytes 4718596
  65.4 1.4 %copy-start.6 = (bf16[24,2,128,128]{3,2,1,0:T(8,128)(2,1)S(1)}, bf16[24,2,128,128]{3,2,1,0:T(8,128)(2,1)}, u32[]{:S(2)}) copy-start(bf16[24,2,128,128]{3,2,1,0:T(8,128)(2,1)} %copy-done.5) | copy-start | bytes 4718596
  66.8 1.9 %copy-start.8 = (f32[24,2,128,128]{3,2,1,0:T(8,128)S(1)}, f32[24,2,128,128]{3,2,1,0:T(8,128)}, u32[]{:S(2)}) copy-start(f32[24,2,128,128]{3,2,1,0:T(8,128)} %copy-done.7) | copy-start | bytes 9437188
  77.3 1.0 copy-start.1
  78.3 16.0 %collective-permute-start.1 = (bf16[4,4,128,128]{3,2,1,0:T(8,128)(2,1)}, bf16[4,4,128,128]{3,2,1,0:T(8,128)(2,1)}, u32[]{:S(2)}, u32[]{:S(2)}) collective-permute-start(bf16[4,4,128,128]{3,2,1,0:T(8,128)(2,1)} %get-tuple-element.24), channel_id=1, source_target_pairs={{24,0},{26,2},{28,4},{30,6},{16,8},{18,10},{20,12},{22,14},{25,1},... | collective-permute-start | bytes 1572872 | tf_op jit(solution)/shard_map/ppermute | solution.py:259
  79.5 20.2 %all-to-all-start.3 = ((bf16[8,4,128,128]{3,2,1,0:T(8,128)(2,1)}), bf16[8,4,128,128]{3,2,1,0:T(8,128)(2,1)S(1)}, u32[]{:S(2)}, u32[]{:S(2)}) async-start(bf16[8,4,128,128]{3,2,1,0:T(8,128)(2,1)} %copy-done), calls=%async_computation.3 | async-start | bytes 2097152 | tf_op jit(solution)/shard_map/all_to_all | solution.py:238
  84.0 11.5 %copy-start.2 = (bf16[8,4,128,128]{3,2,1,0:T(8,128)(2,1)S(1)}, bf16[8,4,128,128]{3,2,1,0:T(8,128)(2,1)}, u32[]{:S(2)}) copy-start(bf16[8,4,128,128]{3,2,1,0:T(8,128)(2,1)} %copy-done.1) | copy-start | bytes 3145732
  99.8 30.6 %all-to-all-start.4 = ((bf16[8,8,128,128]{3,2,1,0:T(8,128)(2,1)}), bf16[8,8,128,128]{3,2,1,0:T(8,128)(2,1)S(1)}, u32[]{:S(2)}, u32[]{:S(2)}) async-start(bf16[8,8,128,128]{3,2,1,0:T(8,128)(2,1)} %maximum_maximum_fusion), calls=%async_computation.4 | async-start | bytes 4194304 | tf_op jit(solution)/shard_map/all_to_all | solution.py:238

commit v3 on v2

--- a/solution.py
+++ b/solution.py
@@ -11,7 +11,8 @@
 SCALING = 168.0 ** (-0.5)
 LOG2E = 1.4426950408889634
 NEG = -1e30
-PIECES = 2
+CUTS = (192, 64)
+TILE = 128
 
 NT = (((1,), (1,)), ((), ()))
 NN = (((1,), (0,)), ((), ()))
@@ -63,47 +64,60 @@
         ),
         in_specs=[SMEM, VMEM, VMEM],
         out_specs=(VMEM, VMEM),
-        compiler_params=pltpu.CompilerParams(vmem_limit_bytes=12 * 1024 * 1024),
+        compiler_params=pltpu.CompilerParams(vmem_limit_bytes=24 * 1024 * 1024),
         cost_estimate=pl.CostEstimate(flops=10**6, bytes_accessed=6 * 2**20, transcendentals=0),
     )(meta, kv, halo)
 
 
-def attention_kernel(*refs, blocks, before, group, piece, first_piece, last_piece):
+def attention_kernel(*refs, blocks, before, group, rows, row0, first_piece, last_piece):
     refs = list(refs)
-    meta_ref, ends_ref, k_ref, kt_ref, x_ref = refs[:5]
+    meta_ref, ends_ref, k_hbm, kt_hbm, x_ref = refs[:5]
     refs = refs[5:]
     if not first_piece:
-        given_ref = refs.pop(0)
-    y_ref = refs.pop(0)
+        given_hbm = refs.pop(0)
+    y_hbm = refs.pop(0)
     if last_piece:
-        dkv_ref, dhalo_ref, acc_ref, s_ref, g_ref = refs
+        dkv_ref, dhalo_ref = refs[:2]
+        refs = refs[2:]
     else:
-        acc_ref, s_ref, g_ref = refs
-    tile, dim = x_ref.shape[2:]
-    wide = group * tile
+        acc_hbm = refs.pop(0)
+    k_ref, kt_ref, acc_ref, s_ref, g_ref, y_ref, k_sem, kt_sem, acc_sem, y_sem = refs[:10]
+    k_copy = pltpu.make_async_copy(k_hbm, k_ref, k_sem)
+    kt_copy = pltpu.make_async_copy(kt_hbm, kt_ref, kt_sem)
+    k_copy.start()
+    kt_copy.start()
+    if not first_piece:
+        given_ref = refs[10]
+        given_copy = pltpu.make_async_copy(given_hbm, given_ref, acc_sem)
+        given_copy.start()
+    part, dim = x_ref.shape[2:]
+    tile = k_ref.shape[2]
+    wide = group * part
     tiles = k_ref.shape[0]
-    cuts = tiles // (blocks + before)
+    cuts = rows // tile
+    final = (row0 + part - 1) // tile
     base, turn = meta_ref[blocks], meta_ref[blocks + 1]
 
     def start_step(t, carry):
-        if first_piece:
-            acc_ref[t] = jnp.zeros(acc_ref.shape[1:], jnp.float32)
-        else:
-            acc_ref[t] = given_ref[t]
+        acc_ref[t] = jnp.zeros(acc_ref.shape[1:], jnp.float32)
         return carry
 
     lax.fori_loop(0, tiles, start_step, 0, unroll=4)
 
-    lane = lax.rem(lax.broadcasted_iota(jnp.int32, (1, wide), 1), tile)
+    lane = lax.rem(lax.broadcasted_iota(jnp.int32, (1, wide), 1), part)
     diff = lane - lax.broadcasted_iota(jnp.int32, (2 * tile, wide), 0)
+    k_copy.wait()
+    kt_copy.wait()
+
+    def y_copy(at):
+        return pltpu.make_async_copy(y_ref.at[at], y_hbm.at[at], y_sem.at[at])
 
     def query_tile(i, count):
-        own = (i + before) * cuts + piece
-        first = own - (count - 1)
+        first = (i + before) * cuts + final - (count - 1)
         at = place(i, turn, blocks)
         q = x_ref[at, 0:group].reshape(wide, dim)
         do = x_ref[at, group:2 * group].reshape(wide, dim)
-        pos = base + (i * cuts + piece) * tile + lane
+        pos = base + i * rows + row0 + lane
         ends = ends_ref[...]
         start = jnp.max(jnp.where(ends <= pos, ends, 0), axis=0, keepdims=True)
         reach = pos - jnp.maximum(start, pos - (WINDOW - 1))
@@ -111,9 +125,9 @@
         top = None
         for a, n in chunks:
             raw = dot(k_ref[pl.ds(first + a, n), 0].reshape(n * tile, dim), q, NT)
-            offset = (count - 1 - a) * tile
+            offset = row0 - (final - (count - 1) + a) * tile
             keep = diff[:n * tile] <= reach - offset
-            if a + n == count:
+            if offset < n * tile - 1:
                 keep = keep & (diff[:n * tile] >= -offset)
             raw = jnp.where(keep, raw, NEG)
             s_ref[a * tile:(a + n) * tile] = raw
@@ -140,68 +154,124 @@
             dq += dot(kt, ds, NN)
             acc_ref[pl.ds(first + a, n), 1] += dot(wb, do, NN).reshape(n, tile, dim)
             acc_ref[pl.ds(first + a, n), 0] += dot(ds, q, NN).reshape(n, tile, dim)
-        for n in range(group):
-            y_ref[at, n] = out[:, n * tile:(n + 1) * tile].T.astype(jnp.bfloat16)
-            y_ref[at, group + n] = (SCALING * dq[:, n * tile:(n + 1) * tile]).T.astype(jnp.bfloat16)
+        y_ref[at, 0:group] = out.T.astype(jnp.bfloat16).reshape(group, part, dim)
+        y_ref[at, group:2 * group] = (SCALING * dq).T.astype(jnp.bfloat16).reshape(group, part, dim)
 
     def query_step(i, carry):
         count = meta_ref[i]
-        for n in range(1, before * cuts + 2):
+        most = final + 1 + (before * rows - row0 - 1) // tile + 1
+        for n in range(1, most + 1):
             pl.when(count == n)(functools.partial(query_tile, i, n))
+        y_copy(place(i, turn, blocks)).start()
         return carry
 
     lax.fori_loop(0, blocks, query_step, 0)
 
     if last_piece:
+        given_copy.wait()
+
         def result(t, c):
-            return SCALING * acc_ref[t * cuts + c, 0], acc_ref[t * cuts + c, 1]
+            both = acc_ref[t * cuts + c] + given_ref[t * cuts + c]
+            return SCALING * both[0], both[1]
 
         def halo_step(t, carry):
             for c in range(cuts):
                 for n, value in enumerate(result(t, c)):
-                    dhalo_ref[t, n * cuts + c] = value.astype(jnp.bfloat16)
+                    dhalo_ref[t, n, c * tile:(c + 1) * tile] = value.astype(jnp.bfloat16)
             return carry
 
         def own_step(t, carry):
             for c in range(cuts):
                 for n, value in enumerate(result(before + t, c)):
-                    dkv_ref[place(t, turn, blocks), n * cuts + c] = value
+                    dkv_ref[place(t, turn, blocks), n, c * tile:(c + 1) * tile] = value
             return carry
 
         lax.fori_loop(0, before, halo_step, 0)
         lax.fori_loop(0, blocks, own_step, 0, unroll=2)
-
-
-def attention(meta, ends, k, kt, x, given, before, piece):
-    blocks, _, tile, dim = x.shape
+    else:
+        acc_copy = pltpu.make_async_copy(acc_ref, acc_hbm, acc_sem)
+        acc_copy.start()
+        acc_copy.wait()
+
+    def wait_step(i, carry):
+        y_copy(i).wait()
+        return carry
+
+    lax.fori_loop(0, blocks, wait_step, 0)
+
+
+def attention(meta, ends, k, kt, x, given, before, rows, row0):
+    blocks, _, part, dim = x.shape
     group = x.shape[1] // 2
-    tiles = k.shape[0]
-    cuts = tiles // (blocks + before)
-    first_piece, last_piece = given is None, piece == PIECES - 1
+    tiles, _, tile, _ = k.shape
+    first_piece, last_piece = given is None, row0 + part == rows
+    hbm = pl.BlockSpec(memory_space=pl.ANY)
     acc = jax.ShapeDtypeStruct((tiles, 2, tile, dim), jnp.float32)
     outs = [jax.ShapeDtypeStruct(x.shape, jnp.bfloat16)]
-    scratch = [pltpu.VMEM(((before * cuts + 1) * tile, group * tile), jnp.float32)] * 2
+    most = (row0 + part - 1) // tile + 2 + (before * rows - row0 - 1) // tile
+    scratch = [
+        pltpu.VMEM(k.shape, k.dtype),
+        pltpu.VMEM(kt.shape, kt.dtype),
+        pltpu.VMEM(acc.shape, acc.dtype),
+        pltpu.VMEM((most * tile, group * part), jnp.float32),
+        pltpu.VMEM((most * tile, group * part), jnp.float32),
+        pltpu.VMEM(x.shape, jnp.bfloat16),
+        pltpu.SemaphoreType.DMA,
+        pltpu.SemaphoreType.DMA,
+        pltpu.SemaphoreType.DMA,
+        pltpu.SemaphoreType.DMA((blocks,)),
+    ]
     if last_piece:
         outs += [
-            jax.ShapeDtypeStruct((blocks, 2 * cuts, tile, dim), jnp.float32),
-            jax.ShapeDtypeStruct((before, 2 * cuts, tile, dim), jnp.bfloat16),
+            jax.ShapeDtypeStruct((blocks, 2, rows, dim), jnp.float32),
+            jax.ShapeDtypeStruct((before, 2, rows, dim), jnp.bfloat16),
         ]
-        scratch = [pltpu.VMEM(acc.shape, acc.dtype)] + scratch
+        scratch.append(pltpu.VMEM(acc.shape, acc.dtype))
     else:
         outs.append(acc)
     operands = [meta, ends, k, kt, x] + ([] if first_piece else [given])
     return pl.pallas_call(
         functools.partial(
-            attention_kernel, blocks=blocks, before=before, group=group, piece=piece,
+            attention_kernel, blocks=blocks, before=before, group=group, rows=rows, row0=row0,
             first_piece=first_piece, last_piece=last_piece,
         ),
         out_shape=tuple(outs),
-        in_specs=[SMEM] + [VMEM] * (len(operands) - 1),
-        out_specs=(VMEM,) * len(outs),
+        in_specs=[SMEM, VMEM, hbm, hbm, VMEM] + [hbm] * (not first_piece),
+        out_specs=(hbm, VMEM, VMEM) if last_piece else (hbm, hbm),
         scratch_shapes=scratch,
-        compiler_params=pltpu.CompilerParams(vmem_limit_bytes=20 * 1024 * 1024),
+        compiler_params=pltpu.CompilerParams(vmem_limit_bytes=60 * 1024 * 1024),
         cost_estimate=pl.CostEstimate(flops=3 * 10**9, bytes_accessed=12 * 2**20, transcendentals=2 * 10**6),
     )(*operands)
+
+
+def combine_kernel(y_ref, dkv_ref, dhalo_ref, out_ref, *, blocks, before, slots):
+    count = y_ref.shape[1]
+    out_ref[0, 0:count] = y_ref[0]
+    behind = pl.program_id(0) >= blocks - before
+    for n in range(2):
+        value = dkv_ref[0, n] + jnp.where(behind, dhalo_ref[0, n].astype(jnp.float32), 0.0)
+        out_ref[0, count + n * slots:count + (n + 1) * slots] = value.astype(out_ref.dtype).reshape(
+            slots, y_ref.shape[2], y_ref.shape[3]
+        )
+
+
+def combine(y, dkv, dhalo):
+    blocks, count, part, dim = y.shape
+    rows, before = dkv.shape[2], dhalo.shape[0]
+    slots = rows // part
+    return pl.pallas_call(
+        functools.partial(combine_kernel, blocks=blocks, before=before, slots=slots),
+        grid=(blocks,),
+        out_shape=jax.ShapeDtypeStruct((blocks, count + 2 * slots, part, dim), y.dtype),
+        in_specs=[
+            pl.BlockSpec((1, count, part, dim), lambda i: (i, 0, 0, 0)),
+            pl.BlockSpec((1, 2, rows, dim), lambda i: (i, 0, 0, 0)),
+            pl.BlockSpec((1, 2, rows, dim), lambda i: (jnp.maximum(i - (blocks - before), 0), 0, 0, 0)),
+        ],
+        out_specs=pl.BlockSpec((1, count + 2 * slots, part, dim), lambda i: (i, 0, 0, 0)),
+        compiler_params=pltpu.CompilerParams(vmem_limit_bytes=60 * 1024 * 1024),
+        cost_estimate=pl.CostEstimate(flops=10**6, bytes_accessed=6 * 2**20, transcendentals=0),
+    )(y, dkv, dhalo)
 
 
 def after(array, other):
@@ -215,7 +285,8 @@
     blocks = kv_heads
     parts = lax.axis_size("ctx") // blocks
     before = WINDOW // rows
-    tile = rows // PIECES
+    tile = TILE
+    starts = [sum(CUTS[:p]) for p in range(len(CUTS))]
     turns = [(p % 2) * (blocks // 2) for p in range(parts)]
     groups = [[p * blocks + (r + turns[p]) % blocks for r in range(blocks)] for p in range(parts)]
     onward = [(groups[p][r], groups[p + 1][r]) for p in range(parts - 1) for r in range(blocks)]
@@ -227,11 +298,12 @@
     base = part * blocks * rows
     turn = lax.rem(part, 2) * (blocks // 2)
     metas = []
-    for piece in range(PIECES):
-        position = base + jnp.arange(blocks, dtype=jnp.int32) * rows + piece * tile
+    for row0, part_rows in zip(starts, CUTS):
+        position = base + jnp.arange(blocks, dtype=jnp.int32) * rows + row0
         start = jnp.max(jnp.where(ends[None, :] <= position[:, None], ends[None, :], 0), axis=1)
         first = jnp.maximum(jnp.maximum(start, position - (WINDOW - 1)), 0)
-        metas.append(jnp.concatenate((position // tile - first // tile + 1, jnp.stack((base, turn)))).astype(jnp.int32))
+        last = (position + part_rows - 1) // tile
+        metas.append(jnp.concatenate((last - first // tile + 1, jnp.stack((base, turn)))).astype(jnp.int32))
     ends = ends[:, None].astype(jnp.int32)
 
     def exchange(array):
@@ -249,19 +321,18 @@
     tail = jnp.stack([kv[(blocks - before + t + turns[0]) % blocks] for t in range(before)]) if turns[0] else kv[blocks - before:]
     halo = lax.ppermute(tail, "ctx", onward)
     packed = [
-        jnp.concatenate([by_head(a[p * tile:(p + 1) * tile]) for a in (queries, out_grad)], 1) for p in range(PIECES)
+        jnp.concatenate([by_head(a[r:r + n]) for a in (queries, out_grad)], 1) for r, n in zip(starts, CUTS)
     ]
-    x0 = exchange(after(packed[0], kv))
+    x0 = exchange(after(packed[0], (kv, packed[1])))
     k, kt = prepare(metas[0], kv, halo, tile)
-    x1 = exchange(after(packed[1], x0))
-    y0, acc = attention(metas[0], ends, k, kt, x0, None, before, 0)
-    y1, dkv, dhalo = attention(metas[1], ends, k, kt, x1, acc, before, 1)
+    x1 = exchange(after(packed[1], (x0, k)))
+    y0, acc = attention(metas[0], ends, k, kt, x0, None, before, rows, starts[0])
+    y1, dkv, dhalo = attention(metas[1], ends, k, kt, x1, acc, before, rows, starts[1])
     dhalo = lax.ppermute(dhalo, "ctx", [(b, a) for a, b in onward])
     y0 = exchange(after(y0, x1))
-    still = blocks - before
-    dkv = jnp.concatenate((dkv[:still], dkv[still:] + dhalo.astype(jnp.float32)), 0).astype(jnp.bfloat16)
-    last = exchange(after(jnp.concatenate((y1, dkv), 1), y0))
-    y1, dk, dv = last[:, :2 * group], last[:, 2 * group:2 * group + PIECES], last[:, 2 * group + PIECES:]
+    last = exchange(after(combine(y1, dkv, dhalo), y0))
+    slots = rows // CUTS[1]
+    y1, dk, dv = last[:, :2 * group], last[:, 2 * group:2 * group + slots], last[:, 2 * group + slots:]
     attended = jnp.concatenate([by_token(y[:, :group]) for y in (y0, y1)], 0)
     query_grad = jnp.concatenate([by_token(y[:, group:]) for y in (y0, y1)], 0)
     dk, dv = (jnp.swapaxes(a.reshape(kv_heads, rows, dim), 0, 1) for a in (dk, dv))

time: 138 us -> 139 us (level)
  Pallas kernels: 18.5 us -> 31.7 us
  local copies, waits for them, and re-layouts: 20 us -> 10.9 us
  other arithmetic: 9.59 us -> 6.34 us
    all_to_all x5, waiting for transfers between devices: 48.7 us -> 35.6 us  [exchange(): return lax.all_to_all(array, 'ctx', 0, 0, axis_index_groups=groups)]
    ppermute x1, waiting for transfers between devices: 0.01 us -> 10 us  [body(): halo = lax.ppermute(tail, 'ctx', onward)]
    pallas_call x2, Pallas kernels: 16.5 us -> 24.4 us  [attention(): pl.pallas_call(functools.partial(attention_kernel, blocks=blocks, before=...]
    unnamed x22 -> x18, local copies, waits for them, and re-layouts: 10.6 us -> 4.02 us
    pallas_call x0 -> x1, Pallas kernels: none -> 5.79 us  [combine(): pl.pallas_call(functools.partial(combine_kernel, blocks=blocks, before=be...]
    ppermute x1, waiting for transfers between devices: 10.2 us -> 14 us  [body(): dhalo = lax.ppermute(dhalo, 'ctx', [(b, a) for a, b in onward])]
    transpose x6 -> x8, local copies, waits for them, and re-layouts: 2.99 us -> 0.86 us  [by_head(): array = jnp.swapaxes(array, 0, 1)]
    concatenate x5 -> x4, other arithmetic: 4.87 us -> 2.79 us  [the longest x2 2.15 us: body(): jnp.concatenate([by_head(a[r:r + n]) for a in (queries, out_grad)], 1)]
  transfers between devices with their start and end apart: 7 -> 7, of which waited for: 6 -> 5; matrix products, arithmetic and copies ran while one was open for 8% -> 4% of each run, Pallas kernels for 7% -> 23%
where the time goes in v3:
time: 139 us; the launch traced here: 138 us
  waiting for transfers between devices  59.6 us (43%)
  Pallas kernels  31.7 us (23%)
  starting transfers between devices  28.3 us (20%)
  local copies, waits for them, and re-layouts  10.9 us (8%)
  other arithmetic  6.34 us (5%)
    all_to_all x5, waiting for transfers between devices, exchange(): return lax.all_to_all(array, 'ctx', 0, 0, axis_index_groups=groups)  35.6 us
    pallas_call x2, Pallas kernels, attention(): pl.pallas_call(functools.partial(attention_kernel, blocks=blocks, before=...  24.4 us
    all_to_all x5, starting transfers between devices, exchange(): return lax.all_to_all(array, 'ctx', 0, 0, axis_index_groups=groups)  22.6 us
    ppermute x1, waiting for transfers between devices, body(): dhalo = lax.ppermute(dhalo, 'ctx', [(b, a) for a, b in onward])  14 us
    ppermute x1, waiting for transfers between devices, body(): halo = lax.ppermute(tail, 'ctx', onward)  10 us
    pallas_call x1, Pallas kernels, combine(): pl.pallas_call(functools.partial(combine_kernel, blocks=blocks, before=be...  5.79 us
    ppermute x1, starting transfers between devices, body(): halo = lax.ppermute(tail, 'ctx', onward)  4.34 us
    unnamed x18, local copies, waits for them, and re-layouts  4.02 us
  transfers between devices with their start and end apart: 7, of which 5 were waited for; matrix products, arithmetic and copies ran while one was open for 4% of the time, Pallas kernels for 23%

profile of v3, /device:TPU:1, one launch (start us, length us, event | category | flops | bytes accessed | tf_op | source)
XLA Modules:
  0.0 137.7 jit_solution(3853034401991433045)
XLA Ops:
  0.6 1.4 %copy_bitcast_fusion.4 = (bf16[8,1,256,128]{3,2,1,0:T(8,128)(2,1)S(1)}, bf16[8,1,256,128]{3,2,1,0:T(8,128)(2,1)S(1)}) fusion(bf16[256,8,128]{2,1,0:T(8,128)(2,1)} %param.7, bf16[256,8,128]{2,1,0:T(8,128)(2,1)} %param.6), kind=kLoop, calls=%fused_computation.11 | loop fusion | bytes 2097152 | tf_op jit(solution)/shard_map/reshape | solution.py:314
  2.0 0.0 copy-start.4
  2.0 1.1 pad_maximum_fusion.1
  3.1 6.5 %all-to-all-start = ((bf16[8,2,256,128]{3,2,1,0:T(8,128)(2,1)}), bf16[8,2,256,128]{3,2,1,0:T(8,128)(2,1)S(1)}, u32[]{:S(2)}, u32[]{:S(2)}) async-start(bf16[8,2,256,128]{3,2,1,0:T(8,128)(2,1)} %pad_maximum_fusion.1), calls=%async_computation | async-start | bytes 2097152 | tf_op jit(solution)/shard_map/all_to_all | solution.py:310
  9.7 0.1 copy.27
  9.8 0.1 copy.28
  9.8 0.1 slice_bitcast_fusion.1
  10.0 0.2 copy.25
  10.2 0.1 slice_bitcast_fusion
  10.3 0.2 copy.26
  10.5 0.8 pad_maximum_fusion.4
  11.4 1.3 pad_maximum_fusion
  12.7 12.7 %all-to-all-done.kv_ref = bf16[8,2,256,128]{3,2,1,0:T(8,128)(2,1)S(1)} async-done(((bf16[8,2,256,128]{3,2,1,0:T(8,128)(2,1)}), bf16[8,2,256,128]{3,2,1,0:T(8,128)(2,1)S(1)}, u32[]{:S(2)}, u32[]{:S(2)}) %all-to-all-start) | async-done | bytes 1048608 | tf_op jit(solution)/shard_map/all_to_all | solution.py:310
  25.4 3.6 %all-to-all-start.1 = ((bf16[8,4,192,128]{3,2,1,0:T(8,128)(2,1)}), bf16[8,4,192,128]{3,2,1,0:T(8,128)(2,1)S(1)}, u32[]{:S(2)}, u32[]{:S(2)}) async-start(bf16[8,4,192,128]{3,2,1,0:T(8,128)(2,1)} %pad_maximum_fusion), calls=%async_computation.1 | async-start | bytes 3145728 | tf_op jit(solution)/shard_map/all_to_all | solution.py:310
  29.0 0.1 select_reduce_fusion
  29.2 4.3 %collective-permute-start = (bf16[4,2,256,128]{3,2,1,0:T(8,128)(2,1)S(1)}, bf16[4,2,256,128]{3,2,1,0:T(8,128)(2,1)S(1)}, u32[]{:S(2)}, u32[]{:S(2)}) collective-permute-start(bf16[4,2,256,128]{3,2,1,0:T(8,128)(2,1)S(1)} %slice.47), channel_id=1, source_target_pairs={{0,24},{2,26},{4,28},{6,30},{8,16},{10,18},{12,20},{14,22},{1,25},... | collective-permute-start | bytes 1572872 | tf_op jit(solution)/shard_map/ppermute | solution.py:322
  33.6 0.2 select_reduce_fusion.2
  33.8 0.1 add_add_fusion.meta_ref.refs_0_
  33.9 10.0 %collective-permute-done.halo_ref = bf16[4,2,256,128]{3,2,1,0:T(8,128)(2,1)S(1)} collective-permute-done((bf16[4,2,256,128]{3,2,1,0:T(8,128)(2,1)S(1)}, bf16[4,2,256,128]{3,2,1,0:T(8,128)(2,1)S(1)}, u32[]{:S(2)}, u32[]{:S(2)}) %collective-permute-start) | collective-permute-done | bytes 524320 | tf_op jit(solution)/shard_map/ppermute | solution.py:322
  43.9 1.5 %shard_map.84 = (bf16[24,2,128,128]{3,2,1,0:T(8,128)(2,1)S(1)}, bf16[24,2,128,128]{3,2,1,0:T(8,128)(2,1)S(1)}) custom-call(s32[10]{0:T(128)S(1)} %add_add_fusion.meta_ref.refs_0_, bf16[8,2,256,128]{3,2,1,0:T(8,128)(2,1)S(1)} %all-to-all-done.kv_ref, bf16[4,2,256,128]{3,2,1,0:T(8,128)(2,1)S(1)} %collective-permute-done.halo_ref), custom_call_target="tpu_custom_call" | custom-call | flops 1000000 | bytes 6291456 | tf_op jit(solution)/shard_map/pallas_call | solution.py:59
  45.4 1.2 copy-done.1
  46.6 1.2 copy-done.2
  47.8 2.6 %all-to-all-done.1.refs_4_ = bf16[8,4,192,128]{3,2,1,0:T(8,128)(2,1)S(1)} async-done(((bf16[8,4,192,128]{3,2,1,0:T(8,128)(2,1)}), bf16[8,4,192,128]{3,2,1,0:T(8,128)(2,1)S(1)}, u32[]{:S(2)}, u32[]{:S(2)}) %all-to-all-start.1) | async-done | bytes 1572896 | tf_op jit(solution)/shard_map/all_to_all | solution.py:310
  50.4 3.5 %all-to-all-start.2 = ((bf16[8,4,64,128]{3,2,1,0:T(8,128)(2,1)}), bf16[8,4,64,128]{3,2,1,0:T(8,128)(2,1)S(1)}, u32[]{:S(2)}, u32[]{:S(2)}) async-start(bf16[8,4,64,128]{3,2,1,0:T(8,128)(2,1)} %pad_maximum_fusion.4), calls=%async_computation.2 | async-start | bytes 1048576 | tf_op jit(solution)/shard_map/all_to_all | solution.py:310
  53.9 0.7 copy.29.refs_1_
  54.6 14.2 %shard_map.85 = (bf16[8,4,192,128]{3,2,1,0:T(8,128)(2,1)}, f32[24,2,128,128]{3,2,1,0:T(8,128)}) custom-call(s32[10]{0:T(128)} %copy-done, s32[32,1]{1,0:T(8,128)} %copy.29.refs_1_, bf16[24,2,128,128]{3,2,1,0:T(8,128)(2,1)} %copy-done.1, bf16[24,2,128,128]{3,2,1,0:T(8,128)(2,1)} %copy-done.2, bf16[8,4,192,128]{3,2,1,0:T(8,128)(2,1)} %copy-done.3), custom_call_target="tpu_custom_call" | custom-call | flops 3000000000 | bytes 12582912 | tf_op jit(solution)/shard_map/pallas_call | solution.py:233
  68.8 0.0 copy-start.7
  68.8 0.8 copy-done.7
  69.6 5.1 %all-to-all-start.3 = ((bf16[8,4,192,128]{3,2,1,0:T(8,128)(2,1)}), bf16[8,4,192,128]{3,2,1,0:T(8,128)(2,1)S(1)}, u32[]{:S(2)}, u32[]{:S(2)}) async-start(bf16[8,4,192,128]{3,2,1,0:T(8,128)(2,1)} %get-tuple-element.20), calls=%async_computation.3 | async-start | bytes 3145728 | tf_op jit(solution)/shard_map/all_to_all | solution.py:310
  74.7 0.6 add_add_fusion.1.refs_0_
  75.3 10.2 %shard_map.86 = (bf16[8,4,64,128]{3,2,1,0:T(8,128)(2,1)}, f32[8,2,256,128]{3,2,1,0:T(8,128)}, bf16[4,2,256,128]{3,2,1,0:T(8,128)(2,1)}) custom-call(s32[10]{0:T(128)} %add_add_fusion.1.refs_0_, s32[32,1]{1,0:T(8,128)} %copy.29.refs_1_, bf16[24,2,128,128]{3,2,1,0:T(8,128)(2,1)} %copy-done.1, bf16[24,2,128,128]{3,2,1,0:T(8,128)(2,1)} %copy-done.2, ...), custom_call_target="tpu_custom_call" | custom-call | flops 3000000000 | bytes 12582912 | tf_op jit(solution)/shard_map/pallas_call | solution.py:233
  85.5 1.3 collective-permute-start.1
  86.8 14.0 %collective-permute-done.1.dhalo_ref = bf16[4,2,256,128]{3,2,1,0:T(8,128)(2,1)S(1)} collective-permute-done((bf16[4,2,256,128]{3,2,1,0:T(8,128)(2,1)}, bf16[4,2,256,128]{3,2,1,0:T(8,128)(2,1)S(1)}, u32[]{:S(2)}, u32[]{:S(2)}) %collective-permute-start.1) | collective-permute-done | bytes 524320 | tf_op jit(solution)/shard_map/ppermute | solution.py:331
  100.8 0.8 copy-done.6
  101.6 5.8 %shard_map.87 = bf16[8,12,64,128]{3,2,1,0:T(8,128)(2,1)} custom-call(bf16[8,4,64,128]{3,2,1,0:T(8,128)(2,1)} %get-tuple-element.22.y_ref, f32[8,2,256,128]{3,2,1,0:T(8,128)} %get-tuple-element.23.dkv_ref, bf16[4,2,256,128]{3,2,1,0:T(8,128)(2,1)} %copy-done.6), custom_call_target="tpu_custom_call" | custom-call | flops 1000000 | bytes 6291456 | tf_op jit(solution)/shard_map/pallas_call | solution.py:262
  107.4 0.0 all-to-all-done.3
  107.4 4.0 %all-to-all-start.4 = ((bf16[8,12,64,128]{3,2,1,0:T(8,128)(2,1)}), bf16[8,12,64,128]{3,2,1,0:T(8,128)(2,1)S(1)}, u32[]{:S(2)}, u32[]{:S(2)}) async-start(bf16[8,12,64,128]{3,2,1,0:T(8,128)(2,1)} %shard_map.87), calls=%async_computation.4 | async-start | bytes 3145728 | tf_op jit(solution)/shard_map/all_to_all | solution.py:310
  111.4 0.1 fusion.1
  111.5 0.5 copy.45
  112.0 0.5 copy.46
  112.5 20.2 %all-to-all-done.4 = bf16[8,12,64,128]{3,2,1,0:T(8,128)(2,1)S(1)} async-done(((bf16[8,12,64,128]{3,2,1,0:T(8,128)(2,1)}), bf16[8,12,64,128]{3,2,1,0:T(8,128)(2,1)S(1)}, u32[]{:S(2)}, u32[]{:S(2)}) %all-to-all-start.4) | async-done | bytes 1572896 | tf_op jit(solution)/shard_map/all_to_all | solution.py:310
  132.8 0.1 fusion
  132.9 1.1 copy.47
  134.0 1.1 copy.48
  135.2 0.2 copy.49
  135.4 0.2 copy.50
  135.6 1.1 pad_maximum_fusion.3
  136.6 1.1 pad_maximum_fusion.2
  (20 shorter events, 0.2 us)
Async XLA Ops:
  2.0 7.6 %copy-start.4 = (bf16[256,16,128]{2,1,0:T(8,128)(2,1)S(1)}, bf16[256,16,128]{2,1,0:T(8,128)(2,1)}, u32[]{:S(2)}) copy-start(bf16[256,16,128]{2,1,0:T(8,128)(2,1)} %param.5) | copy-start | bytes 3145732
  3.1 6.5 %copy-start.5 = (bf16[256,16,128]{2,1,0:T(8,128)(2,1)S(1)}, bf16[256,16,128]{2,1,0:T(8,128)(2,1)}, u32[]{:S(2)}) copy-start(bf16[256,16,128]{2,1,0:T(8,128)(2,1)} %param.8) | copy-start | bytes 3145732
  3.1 22.3 %all-to-all-start = ((bf16[8,2,256,128]{3,2,1,0:T(8,128)(2,1)}), bf16[8,2,256,128]{3,2,1,0:T(8,128)(2,1)S(1)}, u32[]{:S(2)}, u32[]{:S(2)}) async-start(bf16[8,2,256,128]{3,2,1,0:T(8,128)(2,1)} %pad_maximum_fusion.1), calls=%async_computation | async-start | bytes 2097152 | tf_op jit(solution)/shard_map/all_to_all | solution.py:310
  12.7 16.3 %copy-start.8 = (s32[32]{0:T(128)S(1)}, s32[32]{0:T(128)}, u32[]{:S(2)}) copy-start(s32[32]{0:T(128)} %param.9) | copy-start | bytes 388
  25.4 25.0 %all-to-all-start.1 = ((bf16[8,4,192,128]{3,2,1,0:T(8,128)(2,1)}), bf16[8,4,192,128]{3,2,1,0:T(8,128)(2,1)S(1)}, u32[]{:S(2)}, u32[]{:S(2)}) async-start(bf16[8,4,192,128]{3,2,1,0:T(8,128)(2,1)} %pad_maximum_fusion), calls=%async_computation.1 | async-start | bytes 3145728 | tf_op jit(solution)/shard_map/all_to_all | solution.py:310
  29.2 14.7 %collective-permute-start = (bf16[4,2,256,128]{3,2,1,0:T(8,128)(2,1)S(1)}, bf16[4,2,256,128]{3,2,1,0:T(8,128)(2,1)S(1)}, u32[]{:S(2)}, u32[]{:S(2)}) collective-permute-start(bf16[4,2,256,128]{3,2,1,0:T(8,128)(2,1)S(1)} %slice.47), channel_id=1, source_target_pairs={{0,24},{2,26},{4,28},{6,30},{8,16},{10,18},{12,20},{14,22},{1,25},... | collective-permute-start | bytes 1572872 | tf_op jit(solution)/shard_map/ppermute | solution.py:322
  33.9 20.7 %copy-start = (s32[10]{0:T(128)}, s32[10]{0:T(128)S(1)}, u32[]{:S(2)}) copy-start(s32[10]{0:T(128)S(1)} %add_add_fusion.meta_ref.refs_0_) | copy-start | bytes 124
  45.4 1.2 copy-start.1
  46.6 1.2 copy-start.2
  50.4 4.2 %copy-start.3 = (bf16[8,4,192,128]{3,2,1,0:T(8,128)(2,1)}, bf16[8,4,192,128]{3,2,1,0:T(8,128)(2,1)S(1)}, u32[]{:S(2)}) copy-start(bf16[8,4,192,128]{3,2,1,0:T(8,128)(2,1)S(1)} %all-to-all-done.1.refs_4_) | copy-start | bytes 4718596
  50.4 18.4 %all-to-all-start.2 = ((bf16[8,4,64,128]{3,2,1,0:T(8,128)(2,1)}), bf16[8,4,64,128]{3,2,1,0:T(8,128)(2,1)S(1)}, u32[]{:S(2)}, u32[]{:S(2)}) async-start(bf16[8,4,64,128]{3,2,1,0:T(8,128)(2,1)} %pad_maximum_fusion.4), calls=%async_computation.2 | async-start | bytes 1048576 | tf_op jit(solution)/shard_map/all_to_all | solution.py:310
  68.8 0.8 copy-start.7
  69.6 37.8 %all-to-all-start.3 = ((bf16[8,4,192,128]{3,2,1,0:T(8,128)(2,1)}), bf16[8,4,192,128]{3,2,1,0:T(8,128)(2,1)S(1)}, u32[]{:S(2)}, u32[]{:S(2)}) async-start(bf16[8,4,192,128]{3,2,1,0:T(8,128)(2,1)} %get-tuple-element.20), calls=%async_computation.3 | async-start | bytes 3145728 | tf_op jit(solution)/shard_map/all_to_all | solution.py:310
  85.5 15.3 %collective-permute-start.1 = (bf16[4,2,256,128]{3,2,1,0:T(8,128)(2,1)}, bf16[4,2,256,128]{3,2,1,0:T(8,128)(2,1)S(1)}, u32[]{:S(2)}, u32[]{:S(2)}) collective-permute-start(bf16[4,2,256,128]{3,2,1,0:T(8,128)(2,1)} %get-tuple-element.24), channel_id=1, source_target_pairs={{24,0},{26,2},{28,4},{30,6},{16,8},{18,10},{20,12},{22,14},{25,1},... | collective-permute-start | bytes 1572872 | tf_op jit(solution)/shard_map/ppermute | solution.py:331
  100.8 0.8 copy-start.6
  107.4 25.4 %all-to-all-start.4 = ((bf16[8,12,64,128]{3,2,1,0:T(8,128)(2,1)}), bf16[8,12,64,128]{3,2,1,0:T(8,128)(2,1)S(1)}, u32[]{:S(2)}, u32[]{:S(2)}) async-start(bf16[8,12,64,128]{3,2,1,0:T(8,128)(2,1)} %shard_map.87), calls=%async_computation.4 | async-start | bytes 3145728 | tf_op jit(solution)/shard_map/all_to_all | solution.py:310

commit v4 on v2

v4 whole, which is shorter than its diff:
```python
import functools

import jax
import jax.numpy as jnp
from jax import lax
from jax.experimental import pallas as pl
from jax.experimental.pallas import tpu as pltpu
from jax.sharding import PartitionSpec as P

WINDOW = 1024
SCALING = 168.0 ** (-0.5)
LOG2E = 1.4426950408889634
NEG = -1e30
TILE = 128
VMEM_LIMIT = 48 * 1024 * 1024

NT = (((1,), (1,)), ((), ()))
NN = (((1,), (0,)), ((), ()))

VMEM = pl.BlockSpec(memory_space=pltpu.VMEM)
SMEM = pl.BlockSpec(memory_space=pltpu.SMEM)


def dot(a, b, dims):
    return lax.dot_general(a, b, dims, preferred_element_type=jnp.float32)


def place(i, turn, blocks):
    return lax.rem(i + turn, blocks)


def prepare_kernel(meta_ref, kv_ref, halo_ref, k_ref, kt_ref, *, blocks, tile):
    before = halo_ref.shape[0]
    cuts = kv_ref.shape[2] // tile
    turn = meta_ref[1]

    def put(source, index, at):
        for n in range(2):
            for c in range(cuts):
                part = source[index, n, c * tile:(c + 1) * tile]
                k_ref[at * cuts + c, n] = part
                kt_ref[at * cuts + c, n] = part.T

    def halo_step(t, carry):
        put(halo_ref, t, t)
        return carry

    def own_step(t, carry):
        put(kv_ref, place(t, turn, blocks), before + t)
        return carry

    lax.fori_loop(0, before, halo_step, 0)
    lax.fori_loop(0, blocks, own_step, 0, unroll=2)


def prepare(meta, kv, halo, tile):
    blocks, _, rows, dim = kv.shape
    tiles = (halo.shape[0] + blocks) * (rows // tile)
    return pl.pallas_call(
        functools.partial(prepare_kernel, blocks=blocks, tile=tile),
        out_shape=(
            jax.ShapeDtypeStruct((tiles, 2, tile, dim), kv.dtype),
            jax.ShapeDtypeStruct((tiles, 2, dim, tile), kv.dtype),
        ),
        in_specs=[SMEM, VMEM, VMEM],
        out_specs=(VMEM, VMEM),
        compiler_params=pltpu.CompilerParams(vmem_limit_bytes=24 * 1024 * 1024),
        cost_estimate=pl.CostEstimate(flops=10**6, bytes_accessed=6 * 2**20, transcendentals=0),
    )(meta, kv, halo)


def attention_kernel(
    meta_ref, ends_ref, k_hbm, kt_hbm, x_ref, y_hbm, dkv_ref, dhalo_ref,
    k_ref, kt_ref, acc_ref, s_ref, g_ref, y_ref, k_sem, kt_sem, y_sem, *, blocks, before, group,
):
    k_copy = pltpu.make_async_copy(k_hbm, k_ref, k_sem)
    kt_copy = pltpu.make_async_copy(kt_hbm, kt_ref, kt_sem)
    k_copy.start()
    kt_copy.start()
    rows, dim = x_ref.shape[2:]
    tile = k_ref.shape[2]
    wide = group * tile
    cuts = rows // tile
    base, turn = meta_ref[blocks * cuts], meta_ref[blocks * cuts + 1]

    def zero_step(t, carry):
        acc_ref[t] = jnp.zeros(acc_ref.shape[1:], jnp.float32)
        return carry

    lax.fori_loop(0, before * cuts, zero_step, 0, unroll=4)

    lane = lax.rem(lax.broadcasted_iota(jnp.int32, (1, wide), 1), tile)
    diff = lane - lax.broadcasted_iota(jnp.int32, (2 * tile, wide), 0)
    k_copy.wait()
    kt_copy.wait()

    def y_copy(at):
        return pltpu.make_async_copy(y_ref.at[at], y_hbm.at[at], y_sem.at[at])

    def query_tile(i, at, piece, count):
        own = before * cuts + i
        first = own - (count - 1)
        span = pl.ds(piece * tile, tile)
        q = x_ref[at, 0:group, span].reshape(wide, dim)
        do = x_ref[at, group:2 * group, span].reshape(wide, dim)
        pos = base + i * tile + lane
        ends = ends_ref[...]
        start = jnp.max(jnp.where(ends <= pos, ends, 0), axis=0, keepdims=True)
        reach = pos - jnp.maximum(start, pos - (WINDOW - 1))
        chunks = [(0, 1)] * (count % 2) + [(a, 2) for a in range(count % 2, count, 2)]
        top = None
        for a, n in chunks:
            raw = dot(k_ref[pl.ds(first + a, n), 0].reshape(n * tile, dim), q, NT)
            offset = (count - 1 - a) * tile
            keep = diff[:n * tile] <= reach - offset
            if a + n == count:
                keep = keep & (diff[:n * tile] >= -offset)
            raw = jnp.where(keep, raw, NEG)
            s_ref[a * tile:(a + n) * tile] = raw
            here = jnp.max(raw, axis=0, keepdims=True)
            top = here if top is None else jnp.maximum(top, here)
            g_ref[a * tile:(a + n) * tile] = dot(k_ref[pl.ds(first + a, n), 1].reshape(n * tile, dim), do, NT)
        total = mixed = 0.0
        for a, n in chunks:
            p = jnp.exp2((s_ref[a * tile:(a + n) * tile] - top) * (SCALING * LOG2E))
            s_ref[a * tile:(a + n) * tile] = p
            total += jnp.sum(p, axis=0, keepdims=True)
            mixed += jnp.sum(p * g_ref[a * tile:(a + n) * tile], axis=0, keepdims=True)
        inverse = 1.0 / total
        row_total = mixed * inverse
        out = dq = 0.0
        for a, n in chunks:
            w = s_ref[a * tile:(a + n) * tile] * inverse
            wb = w.astype(jnp.bfloat16)
            ds = (w * (g_ref[a * tile:(a + n) * tile] - row_total)).astype(jnp.bfloat16)
            kt, vt = (
                jnp.concatenate([kt_ref[first + a + c, m] for c in range(n)], axis=1) for m in range(2)
            )
            out += dot(vt, wb, NN)
            dq += dot(kt, ds, NN)
            for m, part in enumerate((dot(ds, q, NN), dot(wb, do, NN))):
                for c in range(n):
                    if a + c == count - 1:
                        acc_ref[own, m] = part[c * tile:]
                    else:
                        acc_ref[first + a + c, m] += part[c * tile:(c + 1) * tile]
        y_ref[at, 0:group, span] = out.T.astype(jnp.bfloat16).reshape(group, tile, dim)
        y_ref[at, group:2 * group, span] = (SCALING * dq).T.astype(jnp.bfloat16).reshape(group, tile, dim)

    def query_step(i, carry):
        block, piece = i // cuts, lax.rem(i, cuts)
        at = place(block, turn, blocks)
        count = meta_ref[i]
        for n in range(1, before * cuts + 2):
            pl.when(count == n)(functools.partial(query_tile, i, at, piece, n))

        @pl.when(piece == cuts - 1)
        def _():
            y_copy(at).start()

        return carry

    lax.fori_loop(0, blocks * cuts, query_step, 0)

    def result(t, c):
        return SCALING * acc_ref[t * cuts + c, 0], acc_ref[t * cuts + c, 1]

    def halo_step(t, carry):
        for c in range(cuts):
            for n, value in enumerate(result(t, c)):
                dhalo_ref[t, n, c * tile:(c + 1) * tile] = value.astype(jnp.bfloat16)
        return carry

    def own_step(t, carry):
        for c in range(cuts):
            for n, value in enumerate(result(before + t, c)):
                dkv_ref[place(t, turn, blocks), n, c * tile:(c + 1) * tile] = value
        return carry

    lax.fori_loop(0, before, halo_step, 0)
    lax.fori_loop(0, blocks, own_step, 0, unroll=2)

    def wait_step(i, carry):
        y_copy(i).wait()
        return carry

    lax.fori_loop(0, blocks, wait_step, 0)


def attention(meta, ends, k, kt, x, before):
    blocks, _, rows, dim = x.shape
    group = x.shape[1] // 2
    tiles, _, tile, _ = k.shape
    cuts = rows // tile
    hbm = pl.BlockSpec(memory_space=pl.ANY)
    most = before * cuts + 1
    return pl.pallas_call(
        functools.partial(attention_kernel, blocks=blocks, before=before, group=group),
        out_shape=(
            jax.ShapeDtypeStruct(x.shape, jnp.bfloat16),
            jax.ShapeDtypeStruct((blocks, 2, rows, dim), jnp.float32),
            jax.ShapeDtypeStruct((before, 2, rows, dim), jnp.bfloat16),
        ),
        in_specs=[SMEM, VMEM, hbm, hbm, VMEM],
        out_specs=(hbm, VMEM, VMEM),
        scratch_shapes=[
            pltpu.VMEM(k.shape, k.dtype),
            pltpu.VMEM(kt.shape, kt.dtype),
            pltpu.VMEM((tiles, 2, tile, dim), jnp.float32),
            pltpu.VMEM((most * tile, group * tile), jnp.float32),
            pltpu.VMEM((most * tile, group * tile), jnp.float32),
            pltpu.VMEM(x.shape, jnp.bfloat16),
            pltpu.SemaphoreType.DMA,
            pltpu.SemaphoreType.DMA,
            pltpu.SemaphoreType.DMA((blocks,)),
        ],
        compiler_params=pltpu.CompilerParams(vmem_limit_bytes=60 * 1024 * 1024),
        cost_estimate=pl.CostEstimate(flops=5 * 10**9, bytes_accessed=12 * 2**20, transcendentals=4 * 10**6),
    )(meta, ends, k, kt, x)


def after(array, other):
    return lax.optimization_barrier((array, other))[0]


def body(queries, keys, values, out_grad, doc_lengths):
    rows, heads, dim = queries.shape
    kv_heads = keys.shape[1]
    group = heads // kv_heads
    blocks = kv_heads
    parts = lax.axis_size("ctx") // blocks
    before = WINDOW // rows
    tile = TILE
    turns = [(p % 2) * (blocks // 2) for p in range(parts)]
    groups = [[p * blocks + (r + turns[p]) % blocks for r in range(blocks)] for p in range(parts)]
    onward = [(groups[p][r], groups[p + 1][r]) for p in range(parts - 1) for r in range(blocks)]
    part = lax.axis_index("ctx") // blocks

    docs = doc_lengths.shape[0]
    upto = jnp.arange(docs)[:, None] >= jnp.arange(docs)[None, :]
    ends = jnp.sum(jnp.where(upto, doc_lengths[None, :], 0), axis=1)
    base = part * blocks * rows
    turn = lax.rem(part, 2) * (blocks // 2)
    position = base + jnp.arange(blocks * (rows // tile), dtype=jnp.int32) * tile
    start = jnp.max(jnp.where(ends[None, :] <= position[:, None], ends[None, :], 0), axis=1)
    first = jnp.maximum(jnp.maximum(start, position - (WINDOW - 1)), 0)
    meta = jnp.concatenate((position // tile - first // tile + 1, jnp.stack((base, turn)))).astype(jnp.int32)
    ends = ends[:, None].astype(jnp.int32)

    def exchange(array):
        return lax.all_to_all(array, "ctx", 0, 0, axis_index_groups=groups)

    def by_head(array):
        array = jnp.swapaxes(array, 0, 1)
        return array.reshape(kv_heads, array.shape[0] // kv_heads, array.shape[1], dim)

    def by_token(array):
        array = array.reshape(array.shape[0] * array.shape[1], array.shape[2], dim)
        return jnp.swapaxes(array, 0, 1)

    kv = exchange(jnp.concatenate((by_head(keys), by_head(values)), 1))
    tail = jnp.stack([kv[(blocks - before + t + turns[0]) % blocks] for t in range(before)]) if turns[0] else kv[blocks - before:]
    halo = lax.ppermute(tail, "ctx", onward)
    packed = jnp.concatenate([by_head(a) for a in (queries, out_grad)], 1)
    x = exchange(after(packed, kv))
    k, kt = prepare(jnp.stack((base, turn)).astype(jnp.int32), kv, halo, tile)
    y, dkv, dhalo = attention(meta, ends, k, kt, x, before)
    dhalo = lax.ppermute(dhalo, "ctx", [(b, a) for a, b in onward])
    y = exchange(y)
    still = blocks - before
    dkv = jnp.concatenate((dkv[:still], dkv[still:] + dhalo.astype(jnp.float32)), 0).astype(jnp.bfloat16)
    dkv = exchange(after(dkv, y))
    dk, dv = (jnp.swapaxes(dkv[:, n], 0, 1) for n in range(2))
    return by_token(y[:, :group]), by_token(y[:, group:]), dk, dv


def solution(mesh):
    spec = P(("dp", "ctx"), "head", None)
    return jax.shard_map(
        body,
        mesh=mesh,
        in_specs=(spec, spec, spec, spec, P("dp")),
        out_specs=(spec, spec, spec, spec),
        check_vma=False,
    )
```

time: 138 us -> 130 us (0.942)
  local copies, waits for them, and re-layouts: 20 us -> 13.5 us
  waiting for transfers between devices: 58.9 us -> 64.9 us
  other arithmetic: 9.59 us -> 5.95 us
  starting transfers between devices: 27.9 us -> 24.7 us
    ppermute x1, waiting for transfers between devices: 0.01 us -> 9.47 us  [body(): halo = lax.ppermute(tail, 'ctx', onward)]
    all_to_all x5 -> x4, waiting for transfers between devices: 48.7 us -> 42.1 us  [exchange(): return lax.all_to_all(array, 'ctx', 0, 0, axis_index_groups=groups)]
    unnamed x22 -> x16, local copies, waits for them, and re-layouts: 10.6 us -> 6 us
    concatenate x5 -> x2, other arithmetic: 6.84 us -> 2.57 us  [the longest x1 1.51 us: body(): packed = jnp.concatenate([by_head(a) for a in (queries, out_grad)], 1)]
    ppermute x1, waiting for transfers between devices: 10.2 us -> 13.4 us  [body(): dhalo = lax.ppermute(dhalo, 'ctx', [(b, a) for a, b in onward])]
    transpose x6 -> x2, local copies, waits for them, and re-layouts: 2.99 us -> 0.54 us  [by_head(): array = jnp.swapaxes(array, 0, 1)]
    all_to_all x5 -> x4, starting transfers between devices: 21.5 us -> 19.1 us  [exchange(): return lax.all_to_all(array, 'ctx', 0, 0, axis_index_groups=groups)]
    reshape x2 -> x0, local copies, waits for them, and re-layouts: 2.28 us -> none  [body(): a.reshape(kv_heads, rows, dim)]
  transfers between devices with their start and end apart: 7 -> 6, of which waited for: 6 -> 6; matrix products, arithmetic and copies ran while one was open for 8% -> 8% of each run, Pallas kernels for 7% -> 1%
where the time goes in v4:
time: 130 us; the launch traced here: 129 us
  waiting for transfers between devices  64.9 us (50%)
  starting transfers between devices  24.7 us (19%)
  Pallas kernels  18.8 us (14%)
  local copies, waits for them, and re-layouts  13.5 us (10%)
  other arithmetic  5.95 us (5%)
    all_to_all x4, waiting for transfers between devices, exchange(): return lax.all_to_all(array, 'ctx', 0, 0, axis_index_groups=groups)  42.1 us
    all_to_all x4, starting transfers between devices, exchange(): return lax.all_to_all(array, 'ctx', 0, 0, axis_index_groups=groups)  19.1 us
    pallas_call x1, Pallas kernels, attention(): pl.pallas_call(functools.partial(attention_kernel, blocks=blocks, before=...  17.4 us
    ppermute x1, waiting for transfers between devices, body(): dhalo = lax.ppermute(dhalo, 'ctx', [(b, a) for a, b in onward])  13.4 us
    ppermute x1, waiting for transfers between devices, body(): halo = lax.ppermute(tail, 'ctx', onward)  9.47 us
    unnamed x16, local copies, waits for them, and re-layouts  6 us
    ppermute x1, starting transfers between devices, body(): halo = lax.ppermute(tail, 'ctx', onward)  4.34 us
    reshape x2, local copies, waits for them, and re-layouts, by_token(): array = array.reshape(array.shape[0] * array.shape[1], array.shape[2], dim)  3.3 us
  transfers between devices with their start and end apart: 6, of which 6 were waited for; matrix products, arithmetic and copies ran while one was open for 8% of the time, Pallas kernels for 1%

profile of v4, /device:TPU:1, one launch (start us, length us, event | category | flops | bytes accessed | tf_op | source)
XLA Modules:
  0.0 128.7 jit_solution(7892213257119830879)
XLA Ops:
  0.6 1.4 %copy_bitcast_fusion.2 = (bf16[8,1,256,128]{3,2,1,0:T(8,128)(2,1)S(1)}, bf16[8,1,256,128]{3,2,1,0:T(8,128)(2,1)S(1)}) fusion(bf16[256,8,128]{2,1,0:T(8,128)(2,1)} %param.7, bf16[256,8,128]{2,1,0:T(8,128)(2,1)} %param.6), kind=kLoop, calls=%fused_computation.9 | loop fusion | bytes 2097152 | tf_op jit(solution)/shard_map/reshape | solution.py:255
  2.0 0.0 copy-start.3
  2.0 1.1 pad_maximum_fusion.1
  3.1 0.0 copy-start.4
  3.1 6.5 %all-to-all-start = ((bf16[8,2,256,128]{3,2,1,0:T(8,128)(2,1)}), bf16[8,2,256,128]{3,2,1,0:T(8,128)(2,1)S(1)}, u32[]{:S(2)}, u32[]{:S(2)}) async-start(bf16[8,2,256,128]{3,2,1,0:T(8,128)(2,1)} %pad_maximum_fusion.1), calls=%async_computation | async-start | bytes 2097152 | tf_op jit(solution)/shard_map/all_to_all | solution.py:251
  9.6 0.0 copy-done.3
  9.6 0.3 copy.20
  9.9 0.0 copy-done.4
  9.9 0.3 copy.21
  10.2 1.5 %pad_maximum_fusion = bf16[8,4,256,128]{3,2,1,0:T(8,128)(2,1)} fusion(bf16[8,2,256,128]{3,2,1,0:T(8,128)(2,1)S(1)} %bitcast.34, bf16[8,2,256,128]{3,2,1,0:T(8,128)(2,1)S(1)} %bitcast.33), kind=kLoop, calls=%fused_computation | loop fusion | flops 1048576 | bytes 4194304 | tf_op jit(solution)/shard_map/concatenate | solution.py:264
  11.7 0.0 copy-start.6
  11.7 13.7 %all-to-all-done.kv_ref = bf16[8,2,256,128]{3,2,1,0:T(8,128)(2,1)S(1)} async-done(((bf16[8,2,256,128]{3,2,1,0:T(8,128)(2,1)}), bf16[8,2,256,128]{3,2,1,0:T(8,128)(2,1)S(1)}, u32[]{:S(2)}, u32[]{:S(2)}) %all-to-all-start) | async-done | bytes 1048608 | tf_op jit(solution)/shard_map/all_to_all | solution.py:251
  25.4 3.6 %all-to-all-start.1 = ((bf16[8,4,256,128]{3,2,1,0:T(8,128)(2,1)}), bf16[8,4,256,128]{3,2,1,0:T(8,128)(2,1)S(1)}, u32[]{:S(2)}, u32[]{:S(2)}) async-start(bf16[8,4,256,128]{3,2,1,0:T(8,128)(2,1)} %pad_maximum_fusion), calls=%async_computation.1 | async-start | bytes 4194304 | tf_op jit(solution)/shard_map/all_to_all | solution.py:251
  29.1 0.0 copy-done.6
  29.1 0.1 select_reduce_fusion
  29.2 0.7 copy.22.ends_ref
  29.9 4.3 %collective-permute-start = (bf16[4,2,256,128]{3,2,1,0:T(8,128)(2,1)S(1)}, bf16[4,2,256,128]{3,2,1,0:T(8,128)(2,1)S(1)}, u32[]{:S(2)}, u32[]{:S(2)}) collective-permute-start(bf16[4,2,256,128]{3,2,1,0:T(8,128)(2,1)S(1)} %slice.29), channel_id=1, source_target_pairs={{0,24},{2,26},{4,28},{6,30},{8,16},{10,18},{12,20},{14,22},{1,25},... | collective-permute-start | bytes 1572872 | tf_op jit(solution)/shard_map/ppermute | solution.py:263
  34.3 0.1 pad_add_fusion.1.meta_ref
  34.4 0.2 select_reduce_fusion.1
  34.6 0.6 pad_add_fusion.meta_ref
  35.1 9.5 %collective-permute-done.halo_ref = bf16[4,2,256,128]{3,2,1,0:T(8,128)(2,1)S(1)} collective-permute-done((bf16[4,2,256,128]{3,2,1,0:T(8,128)(2,1)S(1)}, bf16[4,2,256,128]{3,2,1,0:T(8,128)(2,1)S(1)}, u32[]{:S(2)}, u32[]{:S(2)}) %collective-permute-start) | collective-permute-done | bytes 524320 | tf_op jit(solution)/shard_map/ppermute | solution.py:263
  44.6 1.5 %shard_map.84 = (bf16[24,2,128,128]{3,2,1,0:T(8,128)(2,1)S(1)}, bf16[24,2,128,128]{3,2,1,0:T(8,128)(2,1)S(1)}) custom-call(s32[2]{0:T(128)S(1)} %pad_add_fusion.1.meta_ref, bf16[8,2,256,128]{3,2,1,0:T(8,128)(2,1)S(1)} %all-to-all-done.kv_ref, bf16[4,2,256,128]{3,2,1,0:T(8,128)(2,1)S(1)} %collective-permute-done.halo_ref), custom_call_target="tpu_custom_call" | custom-call | flops 1000000 | bytes 6291456 | tf_op jit(solution)/shard_map/pallas_call | solution.py:59
  46.1 0.0 copy-start
  46.1 1.1 copy-done
  47.2 0.0 copy-start.1
  47.2 1.2 copy-done.1
  48.5 7.6 %all-to-all-done.1.x_ref = bf16[8,4,256,128]{3,2,1,0:T(8,128)(2,1)S(1)} async-done(((bf16[8,4,256,128]{3,2,1,0:T(8,128)(2,1)}), bf16[8,4,256,128]{3,2,1,0:T(8,128)(2,1)S(1)}, u32[]{:S(2)}, u32[]{:S(2)}) %all-to-all-start.1) | async-done | bytes 2097184 | tf_op jit(solution)/shard_map/all_to_all | solution.py:251
  56.0 0.0 copy-start.2
  56.0 1.3 %copy-done.2 = bf16[8,4,256,128]{3,2,1,0:T(8,128)(2,1)} copy-done((bf16[8,4,256,128]{3,2,1,0:T(8,128)(2,1)}, bf16[8,4,256,128]{3,2,1,0:T(8,128)(2,1)S(1)}, u32[]{:S(2)}) %copy-start.2) | copy-done | bytes 2097176
  57.4 17.4 %shard_map.85 = (bf16[8,4,256,128]{3,2,1,0:T(8,128)(2,1)}, f32[8,2,256,128]{3,2,1,0:T(8,128)}, bf16[4,2,256,128]{3,2,1,0:T(8,128)(2,1)}) custom-call(s32[18]{0:T(128)} %pad_add_fusion.meta_ref, s32[32,1]{1,0:T(8,128)} %copy.22.ends_ref, bf16[24,2,128,128]{3,2,1,0:T(8,128)(2,1)} %copy-done, bf16[24,2,128,128]{3,2,1,0:T(8,128)(2,1)} %copy-done.1, ...), custom_call_target="tpu_custom_call" | custom-call | flops 5000000000 | bytes 12582912 | tf_op jit(solution)/shard_map/pallas_call | solution.py:197
  74.7 0.0 copy-start.5
  74.8 5.2 %all-to-all-start.2 = ((bf16[8,4,256,128]{3,2,1,0:T(8,128)(2,1)}), bf16[8,4,256,128]{3,2,1,0:T(8,128)(2,1)S(1)}, u32[]{:S(2)}, u32[]{:S(2)}) async-start(bf16[8,4,256,128]{3,2,1,0:T(8,128)(2,1)} %get-tuple-element.14), calls=%async_computation.2 | async-start | bytes 4194304 | tf_op jit(solution)/shard_map/all_to_all | solution.py:251
  80.0 0.0 copy-done.5
  80.0 1.3 %collective-permute-start.1 = (bf16[4,2,256,128]{3,2,1,0:T(8,128)(2,1)S(1)}, bf16[4,2,256,128]{3,2,1,0:T(8,128)(2,1)S(1)}, u32[]{:S(2)}, u32[]{:S(2)}) collective-permute-start(bf16[4,2,256,128]{3,2,1,0:T(8,128)(2,1)S(1)} %copy-done.5), channel_id=1, source_target_pairs={{24,0},{26,2},{28,4},{30,6},{16,8},{18,10},{20,12},{22,14},{25,1},... | collective-permute-start | bytes 1572872 | tf_op jit(solution)/shard_map/ppermute | solution.py:268
  81.3 1.3 %slice.39 = bf16[4,2,256,128]{3,2,1,0:T(8,128)(2,1)S(1)} slice(f32[8,2,256,128]{3,2,1,0:T(8,128)} %get-tuple-element.15), slice={[0:4], [0:2], [0:256], [0:128]} | slice | bytes 1048576 | tf_op jit(solution)/shard_map/slice | solution.py:271
  82.6 13.4 %collective-permute-done.1 = bf16[4,2,256,128]{3,2,1,0:T(8,128)(2,1)S(1)} collective-permute-done((bf16[4,2,256,128]{3,2,1,0:T(8,128)(2,1)S(1)}, bf16[4,2,256,128]{3,2,1,0:T(8,128)(2,1)S(1)}, u32[]{:S(2)}, u32[]{:S(2)}) %collective-permute-start.1) | collective-permute-done | bytes 524320 | tf_op jit(solution)/shard_map/ppermute | solution.py:268
  96.0 1.3 %add_convert_fusion = bf16[4,2,256,128]{3,2,1,0:T(8,128)(2,1)S(1)} fusion(bf16[4,2,256,128]{3,2,1,0:T(8,128)(2,1)S(1)} %collective-permute-done.1, f32[8,2,256,128]{3,2,1,0:T(8,128)} %get-tuple-element.15), kind=kLoop, calls=%fused_computation.6 | loop fusion | flops 786432 | bytes 2097152 | tf_op jit(solution)/shard_map/convert.1
  97.3 1.1 pad_maximum_fusion.2
  98.4 8.6 %all-to-all-done.2 = bf16[8,4,256,128]{3,2,1,0:T(8,128)(2,1)S(1)} async-done(((bf16[8,4,256,128]{3,2,1,0:T(8,128)(2,1)}), bf16[8,4,256,128]{3,2,1,0:T(8,128)(2,1)S(1)}, u32[]{:S(2)}, u32[]{:S(2)}) %all-to-all-start.2) | async-done | bytes 2097184 | tf_op jit(solution)/shard_map/all_to_all | solution.py:251
  107.0 3.7 %all-to-all-start.3 = ((bf16[8,2,256,128]{3,2,1,0:T(8,128)(2,1)}), bf16[8,2,256,128]{3,2,1,0:T(8,128)(2,1)S(1)}, u32[]{:S(2)}, u32[]{:S(2)}) async-start(bf16[8,2,256,128]{3,2,1,0:T(8,128)(2,1)} %pad_maximum_fusion.2), calls=%async_computation.3 | async-start | bytes 2097152 | tf_op jit(solution)/shard_map/all_to_all | solution.py:251
  110.8 0.1 fusion
  110.9 1.6 %copy.31 = bf16[16,256,128]{2,0,1:T(8,128)(2,1)} copy(bf16[16,256,128]{2,1,0:T(8,128)(2,1)S(1)} %bitcast.32) | data formatting | bytes 2097152 | tf_op jit(solution)/shard_map/reshape | solution.py:258
  112.6 1.6 %copy.32 = bf16[16,256,128]{2,0,1:T(8,128)(2,1)} copy(bf16[16,256,128]{2,1,0:T(8,128)(2,1)S(1)} %bitcast.31) | data formatting | bytes 2097152 | tf_op jit(solution)/shard_map/reshape | solution.py:258
  114.2 12.1 %all-to-all-done.3 = bf16[8,2,256,128]{3,2,1,0:T(8,128)(2,1)S(1)} async-done(((bf16[8,2,256,128]{3,2,1,0:T(8,128)(2,1)}), bf16[8,2,256,128]{3,2,1,0:T(8,128)(2,1)S(1)}, u32[]{:S(2)}, u32[]{:S(2)}) %all-to-all-start.3) | async-done | bytes 1048608 | tf_op jit(solution)/shard_map/all_to_all | solution.py:251
  126.3 0.1 slice_bitcast_fusion
  126.4 1.1 copy.26
  127.6 1.1 copy.25
  (3 shorter events, 0.1 us)
Async XLA Ops:
  2.0 7.6 %copy-start.3 = (bf16[256,16,128]{2,1,0:T(8,128)(2,1)S(1)}, bf16[256,16,128]{2,1,0:T(8,128)(2,1)}, u32[]{:S(2)}) copy-start(bf16[256,16,128]{2,1,0:T(8,128)(2,1)} %param.5) | copy-start | bytes 3145732
  3.1 6.8 %copy-start.4 = (bf16[256,16,128]{2,1,0:T(8,128)(2,1)S(1)}, bf16[256,16,128]{2,1,0:T(8,128)(2,1)}, u32[]{:S(2)}) copy-start(bf16[256,16,128]{2,1,0:T(8,128)(2,1)} %param.8) | copy-start | bytes 3145732
  3.1 22.3 %all-to-all-start = ((bf16[8,2,256,128]{3,2,1,0:T(8,128)(2,1)}), bf16[8,2,256,128]{3,2,1,0:T(8,128)(2,1)S(1)}, u32[]{:S(2)}, u32[]{:S(2)}) async-start(bf16[8,2,256,128]{3,2,1,0:T(8,128)(2,1)} %pad_maximum_fusion.1), calls=%async_computation | async-start | bytes 2097152 | tf_op jit(solution)/shard_map/all_to_all | solution.py:251
  11.7 17.4 %copy-start.6 = (s32[32]{0:T(128)S(1)}, s32[32]{0:T(128)}, u32[]{:S(2)}) copy-start(s32[32]{0:T(128)} %param.9) | copy-start | bytes 388
  25.4 30.6 %all-to-all-start.1 = ((bf16[8,4,256,128]{3,2,1,0:T(8,128)(2,1)}), bf16[8,4,256,128]{3,2,1,0:T(8,128)(2,1)S(1)}, u32[]{:S(2)}, u32[]{:S(2)}) async-start(bf16[8,4,256,128]{3,2,1,0:T(8,128)(2,1)} %pad_maximum_fusion), calls=%async_computation.1 | async-start | bytes 4194304 | tf_op jit(solution)/shard_map/all_to_all | solution.py:251
  29.9 14.7 %collective-permute-start = (bf16[4,2,256,128]{3,2,1,0:T(8,128)(2,1)S(1)}, bf16[4,2,256,128]{3,2,1,0:T(8,128)(2,1)S(1)}, u32[]{:S(2)}, u32[]{:S(2)}) collective-permute-start(bf16[4,2,256,128]{3,2,1,0:T(8,128)(2,1)S(1)} %slice.29), channel_id=1, source_target_pairs={{0,24},{2,26},{4,28},{6,30},{8,16},{10,18},{12,20},{14,22},{1,25},... | collective-permute-start | bytes 1572872 | tf_op jit(solution)/shard_map/ppermute | solution.py:263
  46.1 1.1 copy-start
  47.2 1.2 copy-start.1
  56.0 1.3 %copy-start.2 = (bf16[8,4,256,128]{3,2,1,0:T(8,128)(2,1)}, bf16[8,4,256,128]{3,2,1,0:T(8,128)(2,1)S(1)}, u32[]{:S(2)}) copy-start(bf16[8,4,256,128]{3,2,1,0:T(8,128)(2,1)S(1)} %all-to-all-done.1.x_ref) | copy-start | bytes 6291460
  74.7 5.2 %copy-start.5 = (bf16[4,2,256,128]{3,2,1,0:T(8,128)(2,1)S(1)}, bf16[4,2,256,128]{3,2,1,0:T(8,128)(2,1)}, u32[]{:S(2)}) copy-start(bf16[4,2,256,128]{3,2,1,0:T(8,128)(2,1)} %get-tuple-element.16) | copy-start | bytes 1572868
  74.8 32.3 %all-to-all-start.2 = ((bf16[8,4,256,128]{3,2,1,0:T(8,128)(2,1)}), bf16[8,4,256,128]{3,2,1,0:T(8,128)(2,1)S(1)}, u32[]{:S(2)}, u32[]{:S(2)}) async-start(bf16[8,4,256,128]{3,2,1,0:T(8,128)(2,1)} %get-tuple-element.14), calls=%async_computation.2 | async-start | bytes 4194304 | tf_op jit(solution)/shard_map/all_to_all | solution.py:251
  80.0 16.0 %collective-permute-start.1 = (bf16[4,2,256,128]{3,2,1,0:T(8,128)(2,1)S(1)}, bf16[4,2,256,128]{3,2,1,0:T(8,128)(2,1)S(1)}, u32[]{:S(2)}, u32[]{:S(2)}) collective-permute-start(bf16[4,2,256,128]{3,2,1,0:T(8,128)(2,1)S(1)} %copy-done.5), channel_id=1, source_target_pairs={{24,0},{26,2},{28,4},{30,6},{16,8},{18,10},{20,12},{22,14},{25,1},... | collective-permute-start | bytes 1572872 | tf_op jit(solution)/shard_map/ppermute | solution.py:268
  107.0 19.3 %all-to-all-start.3 = ((bf16[8,2,256,128]{3,2,1,0:T(8,128)(2,1)}), bf16[8,2,256,128]{3,2,1,0:T(8,128)(2,1)S(1)}, u32[]{:S(2)}, u32[]{:S(2)}) async-start(bf16[8,2,256,128]{3,2,1,0:T(8,128)(2,1)} %pad_maximum_fusion.2), calls=%async_computation.3 | async-start | bytes 2097152 | tf_op jit(solution)/shard_map/all_to_all | solution.py:251

commit v5 on v4

v5 whole, which is shorter than its diff:
```python
import functools

import jax
import jax.numpy as jnp
from jax import lax
from jax.experimental import pallas as pl
from jax.experimental.pallas import tpu as pltpu
from jax.sharding import PartitionSpec as P

WINDOW = 1024
SCALING = 168.0 ** (-0.5)
LOG2E = 1.4426950408889634
NEG = -1e30
TILE = 128
VMEM_LIMIT = 48 * 1024 * 1024
HBM = pl.ANY
JOINT = (2, 6)

NT = (((1,), (1,)), ((), ()))
NN = (((1,), (0,)), ((), ()))

VMEM = pl.BlockSpec(memory_space=pltpu.VMEM)
SMEM = pl.BlockSpec(memory_space=pltpu.SMEM)


def dot(a, b, dims):
    return lax.dot_general(a, b, dims, preferred_element_type=jnp.float32)


def place(i, turn, blocks):
    return lax.rem(i + turn, blocks)


def prepare_kernel(meta_ref, kv_ref, halo_ref, k_hbm, kt_hbm, k_ref, kt_ref, k_sem, kt_sem, *, blocks, tile):
    before = halo_ref.shape[0]
    cuts = kv_ref.shape[2] // tile
    turn = meta_ref[1]

    def put(source, index, at):
        for n in range(2):
            for c in range(cuts):
                part = source[index, n, c * tile:(c + 1) * tile]
                k_ref[at * cuts + c, n] = part
                kt_ref[at * cuts + c, n] = part.T

    def halo_step(t, carry):
        put(halo_ref, t, t)
        return carry

    def own_step(t, carry):
        put(kv_ref, place(t, turn, blocks), before + t)
        return carry

    lax.fori_loop(0, before, halo_step, 0)
    lax.fori_loop(0, blocks, own_step, 0, unroll=2)
    copies = [pltpu.make_async_copy(k_ref, k_hbm, k_sem), pltpu.make_async_copy(kt_ref, kt_hbm, kt_sem)]
    for copy in copies:
        copy.start()
    for copy in copies:
        copy.wait()


def prepare(meta, kv, halo, tile):
    blocks, _, rows, dim = kv.shape
    tiles = (halo.shape[0] + blocks) * (rows // tile)
    outs = (
        jax.ShapeDtypeStruct((tiles, 2, tile, dim), kv.dtype),
        jax.ShapeDtypeStruct((tiles, 2, dim, tile), kv.dtype),
    )
    hbm = pl.BlockSpec(memory_space=HBM)
    return pl.pallas_call(
        functools.partial(prepare_kernel, blocks=blocks, tile=tile),
        out_shape=outs,
        in_specs=[SMEM, VMEM, VMEM],
        out_specs=(hbm, hbm),
        scratch_shapes=[pltpu.VMEM(o.shape, o.dtype) for o in outs] + [pltpu.SemaphoreType.DMA] * 2,
        compiler_params=pltpu.CompilerParams(vmem_limit_bytes=12 * 1024 * 1024),
        cost_estimate=pl.CostEstimate(flops=10**6, bytes_accessed=6 * 2**20, transcendentals=0),
    )(meta, kv, halo)


def attention_kernel(
    meta_ref, ends_ref, k_hbm, kt_hbm, x_hbm, y_hbm, acc_hbm,
    k_ref, kt_ref, x_ref, acc_ref, s_ref, g_ref, y_ref, k_sem, kt_sem, x_sem, y_sem, acc_sem, *, blocks, before, group,
):
    rows, dim = x_ref.shape[2:]
    tile = k_ref.shape[2]
    wide = group * tile
    cuts = rows // tile
    halo = before * cuts
    base, turn = meta_ref[blocks * cuts], meta_ref[blocks * cuts + 1]

    def tile_copies(block):
        near = pl.ds(halo + block * cuts, cuts)
        return [pltpu.make_async_copy(h.at[near], r.at[near], sem.at[block]) for h, r, sem in sources]

    sources = ((k_hbm, k_ref, k_sem), (kt_hbm, kt_ref, kt_sem))
    start_copies = [
        pltpu.make_async_copy(h.at[pl.ds(0, halo + cuts)], r.at[pl.ds(0, halo + cuts)], sem.at[0]) for h, r, sem in sources
    ]

    def x_copy(at):
        return pltpu.make_async_copy(x_hbm.at[at], x_ref.at[at], x_sem.at[at])

    x_copy(place(0, turn, blocks)).start()
    for copy in start_copies:
        copy.start()

    def fetch_step(block, carry):
        x_copy(place(block, turn, blocks)).start()
        for copy in tile_copies(block):
            copy.start()
        return carry

    lax.fori_loop(1, blocks, fetch_step, 0)

    def zero_step(t, carry):
        acc_ref[t] = jnp.zeros(acc_ref.shape[1:], jnp.float32)
        return carry

    lax.fori_loop(0, before, zero_step, 0)

    def acc_at(t, m):
        return t // cuts, m, pl.ds(pl.multiple_of(lax.rem(t, cuts) * tile, tile), tile)

    lane = lax.rem(lax.broadcasted_iota(jnp.int32, (1, wide), 1), tile)
    diff = lane - lax.broadcasted_iota(jnp.int32, (2 * tile, wide), 0)

    def y_copy(at):
        return pltpu.make_async_copy(y_ref.at[at], y_hbm.at[at], y_sem.at[at])

    def acc_copy(t):
        return pltpu.make_async_copy(acc_ref.at[t], acc_hbm.at[t], acc_sem.at[t])

    def scores(slot, i, at, piece, count):
        first = halo + i - (count - 1)
        span = pl.ds(piece * tile, tile)
        q = x_ref[at, 0:group, span].reshape(wide, dim)
        do = x_ref[at, group:2 * group, span].reshape(wide, dim)
        pos = base + i * tile + lane
        ends = ends_ref[...]
        start = jnp.max(jnp.where(ends <= pos, ends, 0), axis=0, keepdims=True)
        reach = pos - jnp.maximum(start, pos - (WINDOW - 1))
        chunks = [(0, 1)] * (count % 2) + [(a, 2) for a in range(count % 2, count, 2)]
        top = None
        for a, n in chunks:
            raw = dot(k_ref[pl.ds(first + a, n), 0].reshape(n * tile, dim), q, NT)
            offset = (count - 1 - a) * tile
            keep = diff[:n * tile] <= reach - offset
            if a + n == count:
                keep = keep & (diff[:n * tile] >= -offset)
            raw = jnp.where(keep, raw, NEG)
            s_ref[slot, a * tile:(a + n) * tile] = raw
            here = jnp.max(raw, axis=0, keepdims=True)
            top = here if top is None else jnp.maximum(top, here)
            g_ref[slot, a * tile:(a + n) * tile] = dot(
                k_ref[pl.ds(first + a, n), 1].reshape(n * tile, dim), do, NT
            )
        return first, q, do, chunks, top

    def weigh(slot, state):
        first, q, do, chunks, top = state
        total = mixed = 0.0
        for a, n in chunks:
            p = jnp.exp2((s_ref[slot, a * tile:(a + n) * tile] - top) * (SCALING * LOG2E))
            s_ref[slot, a * tile:(a + n) * tile] = p
            total += jnp.sum(p, axis=0, keepdims=True)
            mixed += jnp.sum(p * g_ref[slot, a * tile:(a + n) * tile], axis=0, keepdims=True)
        inverse = 1.0 / total
        return first, q, do, chunks, inverse, mixed * inverse

    def gradients(slot, at, piece, count, state):
        first, q, do, chunks, inverse, row_total = state
        span = pl.ds(piece * tile, tile)
        out = dq = 0.0
        for a, n in chunks:
            w = s_ref[slot, a * tile:(a + n) * tile] * inverse
            wb = w.astype(jnp.bfloat16)
            ds = (w * (g_ref[slot, a * tile:(a + n) * tile] - row_total)).astype(jnp.bfloat16)
            kt, vt = (
                jnp.concatenate([kt_ref[first + a + c, m] for c in range(n)], axis=1) for m in range(2)
            )
            out += dot(vt, wb, NN)
            dq += dot(kt, ds, NN)
            for m, part in enumerate((dot(ds, q, NN), dot(wb, do, NN))):
                for c in range(n):
                    here = acc_at(first + a + c, m)
                    if a + c == count - 1:
                        acc_ref[here] = part[c * tile:]
                    else:
                        acc_ref[here] += part[c * tile:(c + 1) * tile]
        y_ref[at, 0:group, span] = out.T.astype(jnp.bfloat16).reshape(group, tile, dim)
        y_ref[at, group:2 * group, span] = (SCALING * dq).T.astype(jnp.bfloat16).reshape(group, tile, dim)

    def query_tiles(block, at, pieces, count):
        states = [scores(slot, block * cuts + c, at, c, count) for slot, c in enumerate(pieces)]
        states = [weigh(slot, state) for slot, state in enumerate(states)]
        for slot, c in enumerate(pieces):
            gradients(slot, at, c, count, states[slot])

    def block_step(block, carry):
        at = place(block, turn, blocks)
        counts = [meta_ref[block * cuts + c] for c in range(cuts)]
        most = functools.reduce(jnp.maximum, counts)
        x_copy(at).wait()

        @pl.when(block == 0)
        def _():
            for copy in start_copies:
                copy.wait()

        @pl.when(block > 0)
        def _():
            for copy in tile_copies(block):
                copy.wait()

        for n in range(JOINT[0], JOINT[1]):
            here = (most == n) if n > JOINT[0] else (most <= n)
            pl.when(here)(functools.partial(query_tiles, block, at, list(range(cuts)), n))
        for c in range(cuts):
            for n in range(1, halo + 2):
                here = (counts[c] == n) & (most >= JOINT[1])
                pl.when(here)(functools.partial(query_tiles, block, at, [c], n))
        y_copy(at).start()
        acc_copy(block).start()
        return carry

    lax.fori_loop(0, blocks, block_step, 0)
    for t in range(blocks, blocks + before):
        acc_copy(t).start()

    def wait_step(i, carry):
        y_copy(i).wait()
        return carry

    def acc_wait_step(t, carry):
        acc_copy(t).wait()
        return carry

    lax.fori_loop(0, blocks, wait_step, 0)
    lax.fori_loop(0, blocks + before, acc_wait_step, 0)


def attention(meta, ends, k, kt, x, before):
    blocks, _, rows, dim = x.shape
    group = x.shape[1] // 2
    tiles, _, tile, _ = k.shape
    cuts = rows // tile
    hbm = pl.BlockSpec(memory_space=HBM)
    any_space = pl.BlockSpec(memory_space=pl.ANY)
    most = before * cuts + 1
    return pl.pallas_call(
        functools.partial(attention_kernel, blocks=blocks, before=before, group=group),
        out_shape=(
            jax.ShapeDtypeStruct(x.shape, jnp.bfloat16),
            jax.ShapeDtypeStruct((before + blocks, 2, rows, dim), jnp.float32),
        ),
        in_specs=[SMEM, VMEM, any_space, any_space, any_space],
        out_specs=(any_space, any_space),
        scratch_shapes=[
            pltpu.VMEM(k.shape, k.dtype),
            pltpu.VMEM(kt.shape, kt.dtype),
            pltpu.VMEM(x.shape, x.dtype),
            pltpu.VMEM((before + blocks, 2, rows, dim), jnp.float32),
            pltpu.VMEM((cuts, most * tile, group * tile), jnp.float32),
            pltpu.VMEM((cuts, most * tile, group * tile), jnp.float32),
            pltpu.VMEM(x.shape, jnp.bfloat16),
            pltpu.SemaphoreType.DMA((blocks,)),
            pltpu.SemaphoreType.DMA((blocks,)),
            pltpu.SemaphoreType.DMA((blocks,)),
            pltpu.SemaphoreType.DMA((blocks,)),
            pltpu.SemaphoreType.DMA((before + blocks,)),
        ],
        compiler_params=pltpu.CompilerParams(vmem_limit_bytes=VMEM_LIMIT),
        cost_estimate=pl.CostEstimate(flops=5 * 10**9, bytes_accessed=12 * 2**20, transcendentals=4 * 10**6),
    )(meta, ends, k, kt, x)


def after(array, other):
    return lax.optimization_barrier((array, other))[0]


def body(queries, keys, values, out_grad, doc_lengths):
    rows, heads, dim = queries.shape
    kv_heads = keys.shape[1]
    group = heads // kv_heads
    blocks = kv_heads
    parts = lax.axis_size("ctx") // blocks
    before = WINDOW // rows
    tile = TILE
    turns = [(p % 2) * (blocks // 2) for p in range(parts)]
    groups = [[p * blocks + (r + turns[p]) % blocks for r in range(blocks)] for p in range(parts)]
    onward = [(groups[p][r], groups[p + 1][r]) for p in range(parts - 1) for r in range(blocks)]
    part = lax.axis_index("ctx") // blocks

    docs = doc_lengths.shape[0]
    upto = jnp.arange(docs)[:, None] >= jnp.arange(docs)[None, :]
    ends = jnp.sum(jnp.where(upto, doc_lengths[None, :], 0), axis=1)
    base = part * blocks * rows
    turn = lax.rem(part, 2) * (blocks // 2)
    position = base + jnp.arange(blocks * (rows // tile), dtype=jnp.int32) * tile
    start = jnp.max(jnp.where(ends[None, :] <= position[:, None], ends[None, :], 0), axis=1)
    first = jnp.maximum(jnp.maximum(start, position - (WINDOW - 1)), 0)
    meta = jnp.concatenate((position // tile - first // tile + 1, jnp.stack((base, turn)))).astype(jnp.int32)
    ends = ends[:, None].astype(jnp.int32)

    def exchange(array):
        return lax.all_to_all(array, "ctx", 0, 0, axis_index_groups=groups)

    def by_head(array):
        array = jnp.swapaxes(array, 0, 1)
        return array.reshape(kv_heads, array.shape[0] // kv_heads, array.shape[1], dim)

    def by_token(array):
        array = array.reshape(array.shape[0] * array.shape[1], array.shape[2], dim)
        return jnp.swapaxes(array, 0, 1)

    kv = exchange(jnp.concatenate((by_head(keys), by_head(values)), 1))
    tail = jnp.stack([kv[(blocks - before + t + turns[0]) % blocks] for t in range(before)]) if turns[0] else kv[blocks - before:]
    halo = lax.ppermute(tail, "ctx", onward)
    packed = jnp.concatenate([by_head(a) for a in (queries, out_grad)], 1)
    x = exchange(after(packed, kv))
    k, kt = prepare(jnp.stack((base, turn)).astype(jnp.int32), kv, halo, tile)
    y, acc = attention(meta, ends, k, kt, x, before)
    acc = acc * jnp.where(jnp.arange(2) == 0, SCALING, 1.0).astype(jnp.float32)[:, None, None]
    dhalo = lax.ppermute(acc[:before].astype(jnp.bfloat16), "ctx", [(b, a) for a, b in onward])
    y = exchange(y)
    half = blocks // 2
    dkv = jnp.concatenate((acc[before:blocks], acc[blocks:] + dhalo.astype(jnp.float32)), 0)
    dkv = jnp.where(turn == 0, dkv, jnp.concatenate((dkv[half:], dkv[:half]), 0)).astype(jnp.bfloat16)
    dkv = exchange(after(dkv, y))
    dk, dv = (jnp.swapaxes(dkv[:, n], 0, 1) for n in range(2))
    return by_token(y[:, :group]), by_token(y[:, group:]), dk, dv


def solution(mesh):
    spec = P(("dp", "ctx"), "head", None)
    return jax.shard_map(
        body,
        mesh=mesh,
        in_specs=(spec, spec, spec, spec, P("dp")),
        out_specs=(spec, spec, spec, spec),
        check_vma=False,
    )
```

time: 130 us -> 130 us (level)
  other arithmetic: 5.95 us -> 7.62 us
    mul x0 -> x1, other arithmetic: none -> 2.28 us  [body(): acc * jnp.where(jnp.arange(2) == 0, SCALING, 1.0).astype(jnp.float32)[:,...]
    all_to_all x4, waiting for transfers between devices: 42.1 us -> 40.3 us  [exchange(): return lax.all_to_all(array, 'ctx', 0, 0, axis_index_groups=groups)]
    slice x1, local copies, waits for them, and re-layouts: 0.14 us -> 1.68 us  [body(): return (by_token(y[:, :group]), by_token(y[:, group:]), dk, dv)]
    another operation x1 -> x0, other arithmetic: 1.33 us -> none
    unnamed x16 -> x14, local copies, waits for them, and re-layouts: 6 us -> 4.85 us
  transfers between devices with their start and end apart: 6 -> 6, of which waited for: 6 -> 6; matrix products, arithmetic and copies ran while one was open for 8% -> 10% of each run, Pallas kernels for 1% -> 1%
where the time goes in v5:
time: 130 us; the launch traced here: 129 us
  waiting for transfers between devices  63.8 us (49%)
  starting transfers between devices  25.2 us (19%)
  Pallas kernels  18.9 us (15%)
  local copies, waits for them, and re-layouts  13.1 us (10%)
  other arithmetic  7.62 us (6%)
    all_to_all x4, waiting for transfers between devices, exchange(): return lax.all_to_all(array, 'ctx', 0, 0, axis_index_groups=groups)  40.3 us
    all_to_all x4, starting transfers between devices, exchange(): return lax.all_to_all(array, 'ctx', 0, 0, axis_index_groups=groups)  19.5 us
    pallas_call x1, Pallas kernels, attention(): pl.pallas_call(functools.partial(attention_kernel, blocks=blocks, before=...  17.2 us
    ppermute x1, waiting for transfers between devices, body(): lax.ppermute(acc[:before].astype(jnp.bfloat16), 'ctx', [(b, a) for a, b i...  13.4 us
    ppermute x1, waiting for transfers between devices, body(): halo = lax.ppermute(tail, 'ctx', onward)  9.99 us
    unnamed x14, local copies, waits for them, and re-layouts  4.85 us
    ppermute x1, starting transfers between devices, body(): halo = lax.ppermute(tail, 'ctx', onward)  4.34 us
    reshape x2, local copies, waits for them, and re-layouts, by_token(): array = array.reshape(array.shape[0] * array.shape[1], array.shape[2], dim)  3.3 us
  transfers between devices with their start and end apart: 6, of which 6 were waited for; matrix products, arithmetic and copies ran while one was open for 10% of the time, Pallas kernels for 1%

profile of v5, /device:TPU:1, one launch (start us, length us, event | category | flops | bytes accessed | tf_op | source)
XLA Modules:
  0.0 129.4 jit_solution(12433746864976289896)
XLA Ops:
  0.6 1.4 %copy_bitcast_fusion.2 = (bf16[8,1,256,128]{3,2,1,0:T(8,128)(2,1)S(1)}, bf16[8,1,256,128]{3,2,1,0:T(8,128)(2,1)S(1)}) fusion(bf16[256,8,128]{2,1,0:T(8,128)(2,1)} %param.7, bf16[256,8,128]{2,1,0:T(8,128)(2,1)} %param.6), kind=kLoop, calls=%fused_computation.11 | loop fusion | bytes 2097152 | tf_op jit(solution)/shard_map/reshape | solution.py:312
  2.0 0.0 copy-start.3
  2.0 1.1 pad_maximum_fusion.1
  3.1 0.0 copy-start.4
  3.1 6.5 %all-to-all-start = ((bf16[8,2,256,128]{3,2,1,0:T(8,128)(2,1)}), bf16[8,2,256,128]{3,2,1,0:T(8,128)(2,1)S(1)}, u32[]{:S(2)}, u32[]{:S(2)}) async-start(bf16[8,2,256,128]{3,2,1,0:T(8,128)(2,1)} %pad_maximum_fusion.1), calls=%async_computation | async-start | bytes 2097152 | tf_op jit(solution)/shard_map/all_to_all | solution.py:308
  9.6 0.0 copy-done.3
  9.6 0.3 copy.21
  9.9 0.0 copy-done.4
  9.9 0.3 copy.20
  10.2 1.5 %pad_maximum_fusion = bf16[8,4,256,128]{3,2,1,0:T(8,128)(2,1)} fusion(bf16[8,2,256,128]{3,2,1,0:T(8,128)(2,1)S(1)} %bitcast.33, bf16[8,2,256,128]{3,2,1,0:T(8,128)(2,1)S(1)} %bitcast.34), kind=kLoop, calls=%fused_computation | loop fusion | flops 1048576 | bytes 4194304 | tf_op jit(solution)/shard_map/concatenate | solution.py:321
  11.7 0.0 copy-start.5
  11.7 13.7 %all-to-all-done.kv_ref = bf16[8,2,256,128]{3,2,1,0:T(8,128)(2,1)S(1)} async-done(((bf16[8,2,256,128]{3,2,1,0:T(8,128)(2,1)}), bf16[8,2,256,128]{3,2,1,0:T(8,128)(2,1)S(1)}, u32[]{:S(2)}, u32[]{:S(2)}) %all-to-all-start) | async-done | bytes 1048608 | tf_op jit(solution)/shard_map/all_to_all | solution.py:308
  25.4 4.4 %all-to-all-start.1 = ((bf16[8,4,256,128]{3,2,1,0:T(8,128)(2,1)}), bf16[8,4,256,128]{3,2,1,0:T(8,128)(2,1)}, u32[]{:S(2)}, u32[]{:S(2)}) async-start(bf16[8,4,256,128]{3,2,1,0:T(8,128)(2,1)} %pad_maximum_fusion), calls=%async_computation.1 | async-start | bytes 4194304 | tf_op jit(solution)/shard_map/all_to_all | solution.py:308
  29.8 0.0 copy-done.5
  29.8 0.1 select_reduce_fusion
  29.9 0.1 copy.22.ends_ref
  30.1 4.3 %collective-permute-start = (bf16[4,2,256,128]{3,2,1,0:T(8,128)(2,1)S(1)}, bf16[4,2,256,128]{3,2,1,0:T(8,128)(2,1)S(1)}, u32[]{:S(2)}, u32[]{:S(2)}) collective-permute-start(bf16[4,2,256,128]{3,2,1,0:T(8,128)(2,1)S(1)} %slice.33), channel_id=1, source_target_pairs={{0,24},{2,26},{4,28},{6,30},{8,16},{10,18},{12,20},{14,22},{1,25},... | collective-permute-start | bytes 1572872 | tf_op jit(solution)/shard_map/ppermute | solution.py:320
  34.4 0.1 pad_add_fusion.1.meta_ref
  34.5 0.2 select_reduce_fusion.1
  34.7 0.1 pad_add_fusion.meta_ref
  34.8 10.0 %collective-permute-done.halo_ref = bf16[4,2,256,128]{3,2,1,0:T(8,128)(2,1)S(1)} collective-permute-done((bf16[4,2,256,128]{3,2,1,0:T(8,128)(2,1)S(1)}, bf16[4,2,256,128]{3,2,1,0:T(8,128)(2,1)S(1)}, u32[]{:S(2)}, u32[]{:S(2)}) %collective-permute-start) | collective-permute-done | bytes 524320 | tf_op jit(solution)/shard_map/ppermute | solution.py:320
  44.8 1.7 %shard_map.84 = (bf16[24,2,128,128]{3,2,1,0:T(8,128)(2,1)S(1)}, bf16[24,2,128,128]{3,2,1,0:T(8,128)(2,1)S(1)}) custom-call(s32[2]{0:T(128)S(1)} %pad_add_fusion.1.meta_ref, bf16[8,2,256,128]{3,2,1,0:T(8,128)(2,1)S(1)} %all-to-all-done.kv_ref, bf16[4,2,256,128]{3,2,1,0:T(8,128)(2,1)S(1)} %collective-permute-done.halo_ref), custom_call_target="tpu_custom_call" | custom-call | flops 1000000 | bytes 6291456 | tf_op jit(solution)/shard_map/pallas_call | solution.py:71
  46.5 0.0 copy-start
  46.5 1.1 copy-done
  47.6 9.2 %all-to-all-done.1.x_hbm = bf16[8,4,256,128]{3,2,1,0:T(8,128)(2,1)} async-done(((bf16[8,4,256,128]{3,2,1,0:T(8,128)(2,1)}), bf16[8,4,256,128]{3,2,1,0:T(8,128)(2,1)}, u32[]{:S(2)}, u32[]{:S(2)}) %all-to-all-start.1) | async-done | bytes 2097184 | tf_op jit(solution)/shard_map/all_to_all | solution.py:308
  56.9 0.0 copy-start.1
  56.9 1.4 %copy-done.1 = bf16[24,2,128,128]{3,2,1,0:T(8,128)(2,1)S(1)} copy-done((bf16[24,2,128,128]{3,2,1,0:T(8,128)(2,1)S(1)}, bf16[24,2,128,128]{3,2,1,0:T(8,128)(2,1)}, u32[]{:S(2)}) %copy-start.1) | copy-done | bytes 1572888
  58.3 17.2 %shard_map.85 = (bf16[8,4,256,128]{3,2,1,0:T(8,128)(2,1)}, f32[12,2,256,128]{3,2,1,0:T(8,128)}) custom-call(s32[18]{0:T(128)S(1)} %pad_add_fusion.meta_ref, s32[32,1]{1,0:T(8,128)S(1)} %copy.22.ends_ref, bf16[24,2,128,128]{3,2,1,0:T(8,128)(2,1)S(1)} %get-tuple-element.10.k_hbm, bf16[24,2,128,128]{3,2,1,0:T(8,128)(2,1)S(1)} %copy-done.1, ...), custom_call_target="tpu_custom_call" | custom-call | flops 5000000000 | bytes 12582912 | tf_op jit(solution)/shard_map/pallas_call | solution.py:252
  75.5 5.1 %all-to-all-start.2 = ((bf16[8,4,256,128]{3,2,1,0:T(8,128)(2,1)}), bf16[8,4,256,128]{3,2,1,0:T(8,128)(2,1)}, u32[]{:S(2)}, u32[]{:S(2)}) async-start(bf16[8,4,256,128]{3,2,1,0:T(8,128)(2,1)} %get-tuple-element.13), calls=%async_computation.2 | async-start | bytes 4194304 | tf_op jit(solution)/shard_map/all_to_all | solution.py:308
  80.6 2.3 %broadcast_multiply_fusion = f32[12,2,256,128]{3,2,1,0:T(8,128)S(1)} fusion(f32[12,2,256,128]{3,2,1,0:T(8,128)} %get-tuple-element.14, f32[2]{0:T(128)S(1)} %compare_select_fusion), kind=kLoop, calls=%fused_computation.3 | loop fusion | flops 786432 | bytes 6291464 | tf_op jit(solution)/shard_map/mul | solution.py:325
  82.9 1.2 fusion.1
  84.1 1.3 collective-permute-start.1
  85.3 0.0 copy-start.2
  85.4 13.4 %collective-permute-done.1 = bf16[4,2,256,128]{3,2,1,0:T(8,128)(2,1)} collective-permute-done((bf16[4,2,256,128]{3,2,1,0:T(8,128)(2,1)}, bf16[4,2,256,128]{3,2,1,0:T(8,128)(2,1)}, u32[]{:S(2)}, u32[]{:S(2)}) %collective-permute-start.1) | collective-permute-done | bytes 524320 | tf_op jit(solution)/shard_map/ppermute | solution.py:326
  98.8 1.1 slice_add_fusion
  100.0 0.0 copy-done.2
  100.0 1.1 fusion
  101.1 6.6 %all-to-all-done.2 = bf16[8,4,256,128]{3,2,1,0:T(8,128)(2,1)} async-done(((bf16[8,4,256,128]{3,2,1,0:T(8,128)(2,1)}), bf16[8,4,256,128]{3,2,1,0:T(8,128)(2,1)}, u32[]{:S(2)}, u32[]{:S(2)}) %all-to-all-start.2) | async-done | bytes 2097184 | tf_op jit(solution)/shard_map/all_to_all | solution.py:308
  107.7 3.6 %all-to-all-start.3 = ((bf16[8,2,256,128]{3,2,1,0:T(8,128)(2,1)}), bf16[8,2,256,128]{3,2,1,0:T(8,128)(2,1)S(1)}, u32[]{:S(2)}, u32[]{:S(2)}) async-start(bf16[8,2,256,128]{3,2,1,0:T(8,128)(2,1)} %fusion), calls=%async_computation.3 | async-start | bytes 2097152 | tf_op jit(solution)/shard_map/all_to_all | solution.py:308
  111.3 1.7 %fusion.2 = (bf16[8,2,256,128]{3,2,1,0:T(8,128)(2,1)S(1)}, bf16[8,2,256,128]{3,2,1,0:T(8,128)(2,1)S(1)}) fusion(bf16[8,4,256,128]{3,2,1,0:T(8,128)(2,1)} %all-to-all-done.2), kind=kLoop, calls=%fused_computation.27 | loop fusion | bytes 4194304 | tf_op jit(solution)/shard_map/slice | solution.py:333
  113.0 1.6 %copy.31 = bf16[16,256,128]{2,0,1:T(8,128)(2,1)} copy(bf16[16,256,128]{2,1,0:T(8,128)(2,1)S(1)} %bitcast.32) | data formatting | bytes 2097152 | tf_op jit(solution)/shard_map/reshape | solution.py:315
  114.6 1.6 %copy.32 = bf16[16,256,128]{2,0,1:T(8,128)(2,1)} copy(bf16[16,256,128]{2,1,0:T(8,128)(2,1)S(1)} %bitcast.31) | data formatting | bytes 2097152 | tf_op jit(solution)/shard_map/reshape | solution.py:315
  116.3 10.8 %all-to-all-done.3 = bf16[8,2,256,128]{3,2,1,0:T(8,128)(2,1)S(1)} async-done(((bf16[8,2,256,128]{3,2,1,0:T(8,128)(2,1)}), bf16[8,2,256,128]{3,2,1,0:T(8,128)(2,1)S(1)}, u32[]{:S(2)}, u32[]{:S(2)}) %all-to-all-start.3) | async-done | bytes 1048608 | tf_op jit(solution)/shard_map/all_to_all | solution.py:308
  127.1 0.1 slice_bitcast_fusion
  127.2 1.1 copy.25
  128.3 1.1 copy.26
  (4 shorter events, 0.1 us)
Async XLA Ops:
  2.0 7.6 %copy-start.3 = (bf16[256,16,128]{2,1,0:T(8,128)(2,1)S(1)}, bf16[256,16,128]{2,1,0:T(8,128)(2,1)}, u32[]{:S(2)}) copy-start(bf16[256,16,128]{2,1,0:T(8,128)(2,1)} %param.8) | copy-start | bytes 3145732
  3.1 6.8 %copy-start.4 = (bf16[256,16,128]{2,1,0:T(8,128)(2,1)S(1)}, bf16[256,16,128]{2,1,0:T(8,128)(2,1)}, u32[]{:S(2)}) copy-start(bf16[256,16,128]{2,1,0:T(8,128)(2,1)} %param.5) | copy-start | bytes 3145732
  3.1 22.3 %all-to-all-start = ((bf16[8,2,256,128]{3,2,1,0:T(8,128)(2,1)}), bf16[8,2,256,128]{3,2,1,0:T(8,128)(2,1)S(1)}, u32[]{:S(2)}, u32[]{:S(2)}) async-start(bf16[8,2,256,128]{3,2,1,0:T(8,128)(2,1)} %pad_maximum_fusion.1), calls=%async_computation | async-start | bytes 2097152 | tf_op jit(solution)/shard_map/all_to_all | solution.py:308
  11.7 18.1 %copy-start.5 = (s32[32]{0:T(128)S(1)}, s32[32]{0:T(128)}, u32[]{:S(2)}) copy-start(s32[32]{0:T(128)} %param.9) | copy-start | bytes 388
  25.4 31.5 %all-to-all-start.1 = ((bf16[8,4,256,128]{3,2,1,0:T(8,128)(2,1)}), bf16[8,4,256,128]{3,2,1,0:T(8,128)(2,1)}, u32[]{:S(2)}, u32[]{:S(2)}) async-start(bf16[8,4,256,128]{3,2,1,0:T(8,128)(2,1)} %pad_maximum_fusion), calls=%async_computation.1 | async-start | bytes 4194304 | tf_op jit(solution)/shard_map/all_to_all | solution.py:308
  30.1 14.7 %collective-permute-start = (bf16[4,2,256,128]{3,2,1,0:T(8,128)(2,1)S(1)}, bf16[4,2,256,128]{3,2,1,0:T(8,128)(2,1)S(1)}, u32[]{:S(2)}, u32[]{:S(2)}) collective-permute-start(bf16[4,2,256,128]{3,2,1,0:T(8,128)(2,1)S(1)} %slice.33), channel_id=1, source_target_pairs={{0,24},{2,26},{4,28},{6,30},{8,16},{10,18},{12,20},{14,22},{1,25},... | collective-permute-start | bytes 1572872 | tf_op jit(solution)/shard_map/ppermute | solution.py:320
  46.5 1.2 copy-start
  56.9 1.4 %copy-start.1 = (bf16[24,2,128,128]{3,2,1,0:T(8,128)(2,1)S(1)}, bf16[24,2,128,128]{3,2,1,0:T(8,128)(2,1)}, u32[]{:S(2)}) copy-start(bf16[24,2,128,128]{3,2,1,0:T(8,128)(2,1)} %copy-done) | copy-start | bytes 4718596
  75.5 32.2 %all-to-all-start.2 = ((bf16[8,4,256,128]{3,2,1,0:T(8,128)(2,1)}), bf16[8,4,256,128]{3,2,1,0:T(8,128)(2,1)}, u32[]{:S(2)}, u32[]{:S(2)}) async-start(bf16[8,4,256,128]{3,2,1,0:T(8,128)(2,1)} %get-tuple-element.13), calls=%async_computation.2 | async-start | bytes 4194304 | tf_op jit(solution)/shard_map/all_to_all | solution.py:308
  84.1 14.8 %collective-permute-start.1 = (bf16[4,2,256,128]{3,2,1,0:T(8,128)(2,1)}, bf16[4,2,256,128]{3,2,1,0:T(8,128)(2,1)}, u32[]{:S(2)}, u32[]{:S(2)}) collective-permute-start(bf16[4,2,256,128]{3,2,1,0:T(8,128)(2,1)} %get-tuple-element.25), channel_id=1, source_target_pairs={{24,0},{26,2},{28,4},{30,6},{16,8},{18,10},{20,12},{22,14},{25,1},... | collective-permute-start | bytes 1572872 | tf_op jit(solution)/shard_map/ppermute | solution.py:326
  85.3 14.6 %copy-start.2 = (bf16[4,2,256,128]{3,2,1,0:T(8,128)(2,1)S(1)}, bf16[4,2,256,128]{3,2,1,0:T(8,128)(2,1)}, u32[]{:S(2)}) copy-start(bf16[4,2,256,128]{3,2,1,0:T(8,128)(2,1)} %get-tuple-element.24) | copy-start | bytes 1572868
  107.7 19.3 %all-to-all-start.3 = ((bf16[8,2,256,128]{3,2,1,0:T(8,128)(2,1)}), bf16[8,2,256,128]{3,2,1,0:T(8,128)(2,1)S(1)}, u32[]{:S(2)}, u32[]{:S(2)}) async-start(bf16[8,2,256,128]{3,2,1,0:T(8,128)(2,1)} %fusion), calls=%async_computation.3 | async-start | bytes 2097152 | tf_op jit(solution)/shard_map/all_to_all | solution.py:308
